TPU v7x, 128 devices: a whole 4x4x4 slice. The times are simulated.
128 devices in a mesh: dp: 4 (over z), index: 32 (over x, y, core).
Axes of the slice: x: 4, y: 4, z: 4, core: 2. Of those that a mesh axis runs over, the one named last changes fastest.
Arguments:
- query_codes: int32 [2048, 64], P(('dp', 'index')), may hold values from 0 to 65535, as said below
- positive_ids: int32 [2048], P(('dp', 'index')), may hold values from 0 to 65535
- negative_ids: int32 [2048, 16], P(('dp', 'index')), may hold values from 0 to 65535, as said below
- bank_codes: bfloat16 [65536, 1024], P('index'), may hold values from -1 to 1, as said below
- bank_emb: bfloat16 [65536, 1024], P('index'), may hold values from -0.1875 to 0.1875
- query_emb: bfloat16 [2048, 1024], P(('dp', 'index')), may hold values from -0.75 to 0.75
- positive_emb: bfloat16 [2048, 1024], P(('dp', 'index')), may hold values from -0.1875 to 0.1875
- head: bfloat16 [1024, 1024], replicated, may hold values from -0.1875 to 0.1875
Outputs:
- mined_ids: int32 [2048, 16], P(('dp', 'index'))
- mined_dist: int32 [2048, 16], P(('dp', 'index'))
- query_grad: bfloat16 [2048, 1024], P(('dp', 'index'))
- positive_grad: bfloat16 [2048, 1024], P(('dp', 'index'))
- head_grad: float32 [1024, 1024], P(('dp', 'index'))
Inputs may be any that keep to these rules, and one draw needn't show every extreme that they name: `query_codes`: each word holds 16 independent code bits in its low 16 bits. `bank_codes`: every entry is +1 or -1. `negative_ids`: the owner of an id is id // 2048. Among the 256 ids of one device, one owner holds exactly 39 and every other owner exactly 7; that busiest owner is the same for all devices of one dp group.
All inputs are finite; a program needn't handle non-finite values.
Results may differ from a plain program's by a relative error of at most 0.015.
Values may be sent and summed in bfloat16 or wider, within the bound.
A program may use at most 128 MiB of HBM per device.

v0:
```python
import jax
import jax.numpy as jnp
from jax import lax
from jax.sharding import PartitionSpec as P

TOPK = 16
NEG = 16
CANDS = 17


INV_TEMP = 50.0
EPSILON = 1e-06
LARGEST_KEY = 2147483647


def unpack_signs(codes):
    shifts = jnp.arange(16, dtype=jnp.int32)
    bitset = jnp.bitwise_and(jnp.right_shift(codes[:, :, None], shifts[None, None, :]), 1)
    return (2 * bitset - 1).reshape(codes.shape[0], -1).astype(jnp.bfloat16)


def smallest_keys(keys, count):
    picked = []
    remaining = keys
    for number in range(count):
        lowest = jnp.min(remaining, axis=1)
        picked.append(lowest)
        remaining = jnp.where(remaining == lowest[:, None], LARGEST_KEY, remaining)
    return jnp.stack(picked, axis=1)


def drop_positive(best_keys, positive_ids, passages):
    is_positive = (best_keys % passages == positive_ids[:, None]).astype(jnp.int32)
    passed = jnp.cumsum(is_positive, axis=1) > 0
    return jnp.where(passed[:, :TOPK], best_keys[:, 1 : TOPK + 1], best_keys[:, :TOPK])


def head_backward(query_emb, positive_emb, negative_rows, head):
    query_count, feature_count = query_emb.shape
    query_z = jnp.dot(query_emb, head, preferred_element_type=jnp.float32)
    positive_z = jnp.dot(positive_emb, head, preferred_element_type=jnp.float32)
    negative_z = jnp.dot(
        negative_rows.reshape(-1, feature_count), head, preferred_element_type=jnp.float32
    )
    negative_z = negative_z.reshape(query_count, NEG, feature_count)
    cand_z = jnp.concatenate([positive_z[:, None, :], negative_z], axis=1)
    query_norm = jnp.sqrt(jnp.sum(query_z * query_z, axis=-1, keepdims=True) + EPSILON)
    cand_norm = jnp.sqrt(jnp.sum(cand_z * cand_z, axis=-1, keepdims=True) + EPSILON)
    query_unit = query_z / query_norm
    cand_unit = cand_z / cand_norm
    logits = INV_TEMP * jnp.einsum("qd,qkd->qk", query_unit, cand_unit)
    weights = jnp.exp(logits)
    softmax_probs = weights / jnp.sum(weights, axis=1, keepdims=True)
    first_mark = (jnp.arange(NEG + 1) == 0).astype(jnp.float32)
    slopes = softmax_probs - first_mark[None, :]
    query_du = INV_TEMP * jnp.einsum("qk,qkd->qd", slopes, cand_unit)
    cand_du = INV_TEMP * slopes[:, :, None] * query_unit[:, None, :]
    query_dz = (
        query_du - query_unit * jnp.sum(query_unit * query_du, axis=-1, keepdims=True)
    ) / query_norm
    cand_dz = (
        cand_du - cand_unit * jnp.sum(cand_unit * cand_du, axis=-1, keepdims=True)
    ) / cand_norm
    query_dz = query_dz.astype(jnp.bfloat16)
    cand_dz = cand_dz.astype(jnp.bfloat16)
    return (query_dz, cand_dz[:, 0, :], cand_dz[:, 1:, :])


def local(
    query_codes, positive_ids, negative_ids, bank_codes, bank_emb, query_emb, positive_emb, head
):
    shards = lax.axis_size("index")
    my_shard = lax.axis_index("index")
    pass_local = bank_codes.shape[0]
    bit_count = bank_codes.shape[1]
    passages = pass_local * shards
    local_queries = query_codes.shape[0]
    feature_count = query_emb.shape[1]
    first_id = my_shard * pass_local
    local_ids = first_id + jnp.arange(pass_local, dtype=jnp.int32)
    sign_bits = unpack_signs(lax.all_gather(query_codes, "index", axis=0, tiled=True))
    products = lax.dot_general(
        sign_bits, bank_codes, (((1,), (1,)), ((), ())), preferred_element_type=jnp.float32
    )
    hamming = ((bit_count - products) * 0.5).astype(jnp.int32)
    keyed = hamming * passages + local_ids[None, :]
    group_best = smallest_keys(keyed, CANDS)
    everyone = lax.all_gather(group_best, "index", axis=1, tiled=True)
    own_rows = lax.dynamic_slice_in_dim(everyone, my_shard * local_queries, local_queries, 0)
    best_keys = smallest_keys(own_rows, CANDS)
    chosen = drop_positive(best_keys, positive_ids, passages)
    mined_ids = chosen % passages
    mined_dist = chosen // passages
    flat_ids = negative_ids.reshape(-1)
    sent_count = flat_ids.shape[0]
    capacity = sent_count // 8 + 7 * sent_count // (8 * shards)
    owner_of = flat_ids // pass_local
    offset = flat_ids - owner_of * pass_local
    owner_hits = (owner_of[:, None] == jnp.arange(shards, dtype=jnp.int32)[None, :]).astype(
        jnp.int32
    )
    position = jnp.sum((jnp.cumsum(owner_hits, axis=0) - 1) * owner_hits, axis=1)
    requests = jnp.zeros((shards, capacity), jnp.int32).at[owner_of, position].set(offset)
    asked_offsets = lax.all_to_all(requests, "index", split_axis=0, concat_axis=0, tiled=True)
    fetched = jnp.take(bank_emb, asked_offsets.reshape(-1), axis=0)
    fetched = fetched.reshape(asked_offsets.shape[0], asked_offsets.shape[1], feature_count)
    returned = lax.all_to_all(fetched, "index", split_axis=0, concat_axis=0, tiled=True)
    negative_rows = returned[owner_of, position].reshape(local_queries, NEG, feature_count)
    query_dz, positive_dz, negative_dz = head_backward(query_emb, positive_emb, negative_rows, head)
    contract_out = (((1,), (1,)), ((), ()))
    query_grad = lax.dot_general(
        query_dz, head, contract_out, preferred_element_type=jnp.float32
    ).astype(jnp.bfloat16)
    positive_grad = lax.dot_general(
        positive_dz, head, contract_out, preferred_element_type=jnp.float32
    ).astype(jnp.bfloat16)
    rows_all = jnp.concatenate(
        [query_emb, positive_emb, negative_rows.reshape(-1, feature_count)], axis=0
    )
    slopes_all = jnp.concatenate(
        [query_dz, positive_dz, negative_dz.reshape(-1, feature_count)], axis=0
    )
    devices = lax.axis_size(("dp", "index"))
    share_rows = feature_count // devices
    summed = lax.psum(
        lax.dot_general(
            rows_all, slopes_all, (((0,), (0,)), ((), ())), preferred_element_type=jnp.float32
        ),
        ("dp", "index"),
    )
    head_grad = lax.dynamic_slice_in_dim(
        summed, lax.axis_index(("dp", "index")) * share_rows, share_rows, 0
    )
    return (mined_ids, mined_dist, query_grad, positive_grad, head_grad)


def solution(mesh):
    placed = (
        P(("dp", "index"), None),
        P(("dp", "index")),
        P(("dp", "index"), None),
        P("index", None),
        P("index", None),
        P(("dp", "index"), None),
        P(("dp", "index"), None),
        P(),
    )
    return jax.shard_map(
        local,
        mesh=mesh,
        in_specs=placed,
        out_specs=(
            P(("dp", "index"), None),
            P(("dp", "index"), None),
            P(("dp", "index"), None),
            P(("dp", "index"), None),
            P(("dp", "index"), None),
        ),
        check_vma=False,
    )
```

profile of v0, /device:TPU:1, one launch (start us, length us, event | category | flops | bytes accessed | tf_op | source)
XLA Modules:
  0.0 342.7 jit_solution(5934972324571131409)
XLA Ops:
  8.2 26.5 %all_gather.6 = s32[512,64]{1,0:T(8,128)S(1)} all-gather(s32[16,64]{1,0:T(8,128)} %param.8), channel_id=1, replica_groups=mesh['dp'=4,'index'=32] {'index'}, dimensions={0}, use_global_device_ids=true | all-gather | bytes 135168 | tf_op jit(solution)/shard_map/all_gather | solution.py:81
  35.3 5.2 %fusion.76 = (s32[512]{0:T(512)S(1)}, s32[512,2048]{1,0:T(8,128)S(1)}) fusion(s32[2048]{0:T(1024)S(1)} %iota_add_fusion, bf16[512,1024]{0,1:T(8,128)(2,1)S(1)} %fusion.17, bf16[2048,1024]{1,0:T(8,128)(2,1)} %param.11), kind=kOutput, calls=%fused_computation.172 | convolution fusion | flops 2153774592 | bytes 9447424 | tf_op jit(solution)/shard_map/dot_general | solution.py:82
  42.1 12.7 %fusion.3 = s32[512]{0:T(512)S(1)} fusion(s32[512,2048]{1,0:T(8,128)S(1)} %get-tuple-element.20, s32[512]{0:T(512)S(1)} %fusion.10, s32[512]{0:T(512)S(1)} %fusion.2, s32[512]{0:T(512)S(1)} %get-tuple-element.19), kind=kLoop, calls=%fused_computation.23 | loop fusion | flops 7339520 | bytes 4202496 | tf_op jit(solution)/shard_map/reduce_min | solution.py:26
  54.8 1.8 fusion.75
  59.8 1.8 fusion.74
  63.3 1.5 fusion.7
  64.8 1.8 fusion.73
  69.8 1.8 fusion.1
  71.7 1.9 stack.130
  74.8 12.7 %scatter_fusion = s32[32,39]{1,0:T(8,128)S(1)} fusion(s32[32,39]{1,0:T(8,128)S(1)} %broadcast_in_dim.55, s32[256]{0:T(256)S(1)} %bitcast.131, s32[256]{0:T(256)S(1)} %get-tuple-element.5), kind=kCustom, calls=%fused_computation.2 | custom fusion | bytes 5120 | tf_op jit(solution)/shard_map/scatter | solution.py:103
  87.5 11.8 %all_to_all.14 = s32[32,1,39]{2,1,0:T(1,128)S(1)} all-to-all(s32[32,1,39]{2,1,0:T(1,128)S(1)} %bitcast.129), channel_id=1, replica_groups=mesh['dp'=4,'index'=32] {'index'}, dimensions={0} | all-to-all | bytes 9984 | tf_op jit(solution)/shard_map/all_to_all | solution.py:104
  100.7 9.4 %gather_fusion = bf16[1248,1024]{1,0:T(8,128)(2,1)} fusion(bf16[2048,1024]{1,0:T(8,128)(2,1)} %param.12, s32[2048]{0:T(1024)S(1)} %pad_clamp_fusion), kind=kCustom, calls=%fused_computation | custom fusion | bytes 5116800 | tf_op jit(solution)/shard_map/jit(_take)/gather | solution.py:105
  110.1 4.3 %gather.10 = bf16[32,39,1024]{2,1,0:T(8,128)(2,1)} reshape(bf16[1248,1024]{1,0:T(8,128)(2,1)} %gather_fusion) | data formatting | bytes 5111808 | tf_op jit(solution)/shard_map/jit(_take)/gather | solution.py:105
  114.4 3.6 %broadcast_select_fusion = bf16[32,39,1024]{2,1,0:T(8,128)(2,1)} fusion(bf16[32,39,1024]{2,1,0:T(8,128)(2,1)} %gather.10, pred[32,39]{1,0:T(8,128)(4,1)S(1)} %compare_and_fusion), kind=kLoop, calls=%fused_computation.30 | loop fusion | flops 1277952 | bytes 5113056 | tf_op jit(solution)/shard_map/jit(_take)/select_n | solution.py:105
  118.0 5.3 %all-to-all-start.1 = ((bf16[32,39,1024]{2,1,0:T(8,128)(2,1)}), bf16[32,39,1024]{2,1,0:T(8,128)(2,1)}, u32[]{:S(2)}, u32[]{:S(2)}) async-start(bf16[32,39,1024]{2,1,0:T(8,128)(2,1)} %broadcast_select_fusion), calls=%async_computation.1 | async-start | bytes 5242880 | tf_op jit(solution)/shard_map/all_to_all | solution.py:107
  126.5 1.6 reshape.289
  129.8 27.5 %all-to-all-done.1 = bf16[32,39,1024]{2,1,0:T(8,128)(2,1)} async-done(((bf16[32,39,1024]{2,1,0:T(8,128)(2,1)}), bf16[32,39,1024]{2,1,0:T(8,128)(2,1)}, u32[]{:S(2)}, u32[]{:S(2)}) %all-to-all-start.1) | async-done | bytes 2555936 | tf_op jit(solution)/shard_map/all_to_all | solution.py:107
  157.3 4.7 %copy.226 = bf16[32,39,1024]{2,0,1:T(8,128)(2,1)} copy(bf16[32,39,1024]{2,1,0:T(8,128)(2,1)} %all-to-all-done.1) | data formatting | bytes 5111808 | tf_op jit(solution)/shard_map/all_to_all | solution.py:107
  162.0 3.3 gather_fusion.1
  169.7 2.7 fusion.24
  173.9 2.1 fusion.18
  176.7 4.1 %fusion.27 = f32[1024,1024]{1,0:T(8,128)} fusion(bf16[256,1024]{1,0:T(8,128)(2,1)S(1)} %gather_fusion.1, bf16[16,1024]{1,0:T(8,128)(2,1)} %param.14, bf16[16,1024]{1,0:T(8,128)(2,1)} %param.13, bf16[256,1024]{1,0:T(8,128)(2,1)S(1)} %bitcast.133, bf16[16,1024]{1,0:T(8,128)(2,1)} %slice_bitcast_fusion, bf16[16,1024]{1,0:T(8,128)(2,1)S(1)} %divide_convert_fusion), kind=kOutput, calls=%fused_computation.72 | convolution fusion | flops 607518720 | bytes 5373952 | tf_op jit(solution)/shard_map/dot_general | solution.py:126
  185.8 2.0 convolution_convert_fusion
  187.9 145.6 %all-reduce.2.cloned.1.call-done = f32[1024,1024]{1,0:T(8,128)} async-done(((f32[1024,1024]{1,0:T(8,128)}), f32[1024,1024]{1,0:T(8,128)}) %all-reduce.2.cloned.1.call-update) | async-done | bytes 4194320 | tf_op jit(solution)/shard_map/psum | solution.py:125
  (141 shorter events, 30.5 us)
Async XLA Ops:
  8.0 115.6 %copy-start = (bf16[1024,1024]{1,0:T(8,128)(2,1)S(1)}, bf16[1024,1024]{1,0:T(8,128)(2,1)}, u32[]{:S(2)}) copy-start(bf16[1024,1024]{1,0:T(8,128)(2,1)} %param.15) | copy-start | bytes 6291460
  8.0 118.5 %all-gather.3.cloned.1.call-start = ((), (), s32[]{:S(2)}) async-start(), calls=%async_computation.3 | async-start | bytes 1622016 | tf_op jit(solution)/shard_map/all_gather | solution.py:88
  68.3 5.3 %copy-start.8 = (s32[16,16]{1,0:T(8,128)S(1)}, s32[16,16]{1,0:T(8,128)}, u32[]{:S(2)}) copy-start(s32[16,16]{1,0:T(8,128)} %param.10) | copy-start | bytes 3076
  114.4 9.1 %copy-start.6 = (bf16[16,1024]{1,0:T(8,128)(2,1)S(1)}, bf16[16,1024]{1,0:T(8,128)(2,1)}, u32[]{:S(2)}) copy-start(bf16[16,1024]{1,0:T(8,128)(2,1)} %param.14) | copy-start | bytes 98308
  118.0 6.6 %copy-start.7 = (bf16[16,1024]{1,0:T(8,128)(2,1)S(1)}, bf16[16,1024]{1,0:T(8,128)(2,1)}, u32[]{:S(2)}) copy-start(bf16[16,1024]{1,0:T(8,128)(2,1)} %param.13) | copy-start | bytes 98308
  118.0 39.3 %all-to-all-start.1 = ((bf16[32,39,1024]{2,1,0:T(8,128)(2,1)}), bf16[32,39,1024]{2,1,0:T(8,128)(2,1)}, u32[]{:S(2)}, u32[]{:S(2)}) async-start(bf16[32,39,1024]{2,1,0:T(8,128)(2,1)} %broadcast_select_fusion), calls=%async_computation.1 | async-start | bytes 5242880 | tf_op jit(solution)/shard_map/all_to_all | solution.py:107
  123.3 210.2 %all-reduce.2.cloned.1.call-start = ((), (), s32[]{:S(2)}) async-start(), calls=%async_computation.2 | async-start | bytes 8388608 | tf_op jit(solution)/shard_map/psum | solution.py:125
  123.6 45.3 %copy-start.17 = (f32[17]{0:T(128)}, f32[17]{0:T(128)S(1)}, u32[]{:S(2)}) copy-start(f32[17]{0:T(128)S(1)} %compare_convert_fusion) | copy-start | bytes 208
  125.1 0.7 copy-start.2
  125.1 0.7 copy-start.11
  129.2 0.5 copy-start.13
  129.5 35.9 %copy-start.15 = (s32[16]{0:T(128)}, s32[16]{0:T(128)S(1)}, u32[]{:S(2)}) copy-start(s32[16]{0:T(128)S(1)} %fusion.43) | copy-start | bytes 196
  162.0 4.7 %copy-start.5 = (f32[16,1,1024]{2,0,1:T(8,128)S(1)}, f32[16,1,1024]{2,0,1:T(8,128)}, u32[]{:S(2)}) copy-start(f32[16,1,1024]{2,0,1:T(8,128)} %convolution_bitcast_fusion) | copy-start | bytes 196612
  165.3 2.7 copy-start.10
  166.1 3.6 %copy-start.9 = (f32[16,1024]{1,0:T(8,128)S(1)}, f32[16,1024]{1,0:T(8,128)}, u32[]{:S(2)}) copy-start(f32[16,1024]{1,0:T(8,128)} %broadcast_divide_fusion) | copy-start | bytes 196612
  167.0 1.0 copy-start.1
  168.0 8.0 %copy-start.3 = (f32[16,1024]{1,0:T(8,128)S(1)}, f32[16,1024]{1,0:T(8,128)}, u32[]{:S(2)}) copy-start(f32[16,1024]{1,0:T(8,128)} %copy-done.2) | copy-start | bytes 196612
  168.0 8.0 %copy-start.12 = (f32[16]{0:T(128)S(1)}, f32[16]{0:T(128)}, u32[]{:S(2)}) copy-start(f32[16]{0:T(128)} %copy-done.11) | copy-start | bytes 196
  172.4 0.9 copy-start.4
  176.6 4.5 %copy-start.14 = (s32[16]{0:T(128)S(1)}, s32[16]{0:T(128)}, u32[]{:S(2)}) copy-start(s32[16]{0:T(128)} %copy-done.13) | copy-start | bytes 196
  176.6 4.6 %copy-start.16 = (s32[16]{0:T(128)S(1)}, s32[16]{0:T(128)}, u32[]{:S(2)}) copy-start(s32[16]{0:T(128)} %copy-done.15) | copy-start | bytes 196
  180.7 3.0 copy-start.18
Sparse Core Ops, SparseCore 0:
  73.7 43.2 all-gather.2
Sparse Core Ops, SparseCore 1:
  180.8 152.6 all-reduce.1
where the time goes:
time: 349 us; the launch traced here: 343 us
  waiting for transfers between devices  173 us (50%)
  local copies, waits for them, and re-layouts  45.8 us (13%)
  other arithmetic  45.8 us (13%)
  blocking collectives  38.4 us (11%)
  matrix products  17.6 us (5%)
  between operations  16.3 us (5%)
  starting transfers between devices  5.52 us (2%)
    psum x1, waiting for transfers between devices, local(): lax.psum(lax.dot_general(rows_all, slopes_all, (((0,), (0,)), ((), ())),...  146 us
    reduce_min x33, other arithmetic, smallest_keys(): lowest = jnp.min(remaining, axis=1)  33.9 us
    all_to_all x1, waiting for transfers between devices, local(): lax.all_to_all(fetched, 'index', split_axis=0, concat_axis=0, tiled=True)  27.5 us
    all_gather x1, blocking collectives, local(): lax.all_gather(query_codes, 'index', axis=0, tiled=True)  26.5 us
    gather x2, local copies, waits for them, and re-layouts, local(): fetched = jnp.take(bank_emb, asked_offsets.reshape(-1), axis=0)  13.7 us
    scatter x1, local copies, waits for them, and re-layouts, local(): jnp.zeros((shards, capacity), jnp.int32).at[owner_of, position].set(offset)  12.7 us
    all_to_all x1, blocking collectives, local(): lax.all_to_all(requests, 'index', split_axis=0, concat_axis=0, tiled=True)  11.8 us
  transfers between devices with their start and end apart: 3, of which 2 were waited for; matrix products, arithmetic and copies ran while one was open for 13% of the time, Pallas kernels for 0%

commit v1 on v0

v1 whole, which is shorter than its diff:
```python
import functools

import jax
import jax.numpy as jnp
from jax import lax
from jax.experimental import pallas as pl
from jax.experimental.pallas import tpu as pltpu
from jax.sharding import PartitionSpec as P

F32 = jnp.float32
BF16 = jnp.bfloat16
MESH = pl.DeviceIdType.MESH
MIB = 1 << 20
GROUP = 32
SIDE = 4
BIG = float(1 << 23)
LAST = (((1,), (1,)), ((), ()))


def iota(shape, dim):
    return lax.broadcasted_iota(jnp.int32, shape, dim)


def dot(a, b, dims=(((1,), (0,)), ((), ()))):
    return lax.dot_general(a, b, dims, preferred_element_type=F32)


def copy_to(src, dst, send_sem, recv_sem, device):
    return pltpu.make_async_remote_copy(
        src_ref=src,
        dst_ref=dst,
        send_sem=send_sem,
        recv_sem=recv_sem,
        device_id=device,
        device_id_type=MESH,
    )


def coords():
    z = lax.axis_index("dp")
    me = lax.axis_index("index")
    x = lax.div(me, 8)
    y = lax.rem(lax.div(me, 2), 4)
    c = lax.rem(me, 2)
    return z, me, x, y, c


def at(x, y, c):
    return x * 8 + y * 2 + c


def group_barrier(z, me, with_z):
    barrier = pltpu.get_barrier_semaphore()

    def greet(k, carry):
        pl.semaphore_signal(
            barrier, inc=1, device_id=(z, lax.rem(me + k, GROUP)), device_id_type=MESH
        )
        return carry

    lax.fori_loop(1, GROUP, greet, 0)
    count = GROUP - 1
    if with_z:
        for k in range(1, SIDE):
            pl.semaphore_signal(
                barrier, inc=1, device_id=(lax.rem(z + k, SIDE), me), device_id_type=MESH
            )
        count += SIDE - 1
    pl.semaphore_wait(barrier, count)


def request_table(pay):
    hi = jnp.floor(pay * (1.0 / 256.0))
    lo = pay - 256.0 * hi
    halves = jnp.concatenate([hi, lo], axis=0).astype(BF16)
    lane_of = iota((128, 256), 0)
    item = iota((128, 256), 1)
    spread = jnp.where(lane_of == 65 + (item & 15), 1.0, 0.0).astype(BF16)
    got = dot(halves, spread)
    ids = 256.0 * got[0:16] + got[16:32]
    ids = jnp.where(iota((16, 256), 0) == (iota((16, 256), 1) >> 4), ids, 0.0)
    id_row = jnp.sum(ids, axis=0, keepdims=True)
    owner_row = jnp.floor(id_row * (1.0 / 2048.0))
    owner_b = jnp.broadcast_to(owner_row, (256, 256))
    owner_t = jnp.transpose(owner_b)
    earlier = iota((256, 256), 0) < iota((256, 256), 1)
    same = jnp.where(owner_b == owner_t, 1.0, 0.0)
    rank = jnp.sum(jnp.where(earlier, same, 0.0), axis=0, keepdims=True)
    slot_row = jnp.where(rank < 7.0, owner_row * 8.0 + rank, 249.0 + rank)
    slot_b = jnp.broadcast_to(slot_row, (288, 256))
    hit = iota((288, 256), 0).astype(F32) == slot_b
    id_col = jnp.sum(jnp.where(hit, jnp.broadcast_to(id_row, (288, 256)) + 1.0, 0.0), axis=1, keepdims=True) - 1.0
    which = jnp.where(iota((256, 128), 1) == (iota((256, 128), 0) >> 4), 1.0, 0.0).astype(BF16)
    owned_by = dot(jnp.where(hit, 1.0, 0.0).astype(BF16), which)
    lane32 = iota((32, 128), 1)
    sub32 = iota((32, 128), 0)
    ext_row = jnp.sum(
        jnp.where(lane32 == sub32 + 96, jnp.broadcast_to(id_col[256:288], (32, 128)), 0.0), axis=0, keepdims=True
    )
    lane16 = iota((16, 128), 1)
    common = jnp.where(
        lane16 < 65, pay, jnp.where(lane16 >= 96, jnp.broadcast_to(ext_row, (16, 128)), 0.0)
    )
    return id_col, owned_by, common


def onehot_rows(rel, count):
    return jnp.where(
        jnp.broadcast_to(rel, (count, 2048)) == iota((count, 2048), 1).astype(F32), 1.0, 0.0
    ).astype(BF16)


def fetch_kernel(
    pay_ref, bank_hbm,
    table_ref, owned_ref, base_ref, ext_ref,
    bank, out_buf, in_buf, bsend, brecv, esend, eown, ecore, s1, r2a, r2b, s2a, s2b, r3a, r3b,
    load_sem, p_send, p_recv, b_send, b_recv, c_sem, x_send, x_recv,
):
    z, me, x, y, c = coords()
    load = pltpu.make_async_copy(bank_hbm, bank, load_sem)
    load.start()
    id_col, owned_by, common = request_table(pay_ref[...])
    owned_ref[...] = owned_by
    lane = iota((32, 8, 128), 2)
    base_cols = jnp.broadcast_to(id_col[0:256], (256, 128)).reshape(32, 8, 128)
    out_buf[:, 0:8, :] = jnp.where(lane == 65, base_cols, jnp.broadcast_to(common[None, 0:8], (32, 8, 128)))
    out_buf[:, 8:16, :] = jnp.broadcast_to(common[None, 8:16], (32, 8, 128))
    group_barrier(z, me, False)

    def p_copy(k):
        peer = lax.rem(me + k, GROUP)
        return copy_to(out_buf.at[peer], in_buf.at[me], p_send.at[peer], p_recv.at[me], (z, peer))

    def p_take(k):
        source = lax.rem(me + GROUP - k, GROUP)
        return copy_to(out_buf.at[source], in_buf.at[source], p_send.at[source], p_recv.at[source], (z, source))

    def b_copy(k):
        peer = lax.rem(me + k, GROUP)
        return copy_to(bsend.at[peer], brecv.at[me], b_send.at[peer], b_recv.at[me], (z, peer))

    def b_take(k):
        source = lax.rem(me + GROUP - k, GROUP)
        return copy_to(bsend.at[source], brecv.at[source], b_send.at[source], b_recv.at[source], (z, source))

    def each(act):
        def step(k, carry):
            act(k)
            return carry

        lax.fori_loop(1, GROUP, step, 0)

    each(lambda k: p_copy(k).start())
    in_buf[me] = out_buf[me]
    each(lambda k: p_take(k).wait_recv())
    load.wait()

    first = (me * 2048).astype(F32)
    asked = in_buf[:, 0:8, :].reshape(256, 128)
    base_rel = jnp.sum(jnp.where(iota((256, 128), 1) == 65, asked, 0.0), axis=1, keepdims=True) - first
    hot = onehot_rows(base_rel, 256)
    for h in range(2):
        part = dot(hot, bank[:, h * 512 : (h + 1) * 512])
        bsend[:, 8 * h : 8 * h + 8, :] = part.reshape(32, 8, 512).astype(BF16)
    each(lambda k: b_copy(k).start())
    brecv[me] = bsend[me]

    def extras(core):
        rows = in_buf[:, 0:1, :].reshape(16, 2, 1, 128)
        mine = jnp.where(core == 0, rows[:, 0], rows[:, 1])
        wide = jnp.broadcast_to(mine, (16, 32, 128))
        keep = iota((16, 32, 128), 2) == iota((16, 32, 128), 1) + 96
        rel = jnp.sum(jnp.where(keep, wide, 0.0), axis=2, keepdims=True).reshape(512, 1) - first
        return dot(onehot_rows(rel, 512), bank[...])

    esend[...] = extras(1 - c).reshape(16, 32, 1024).astype(BF16)
    core_copy = copy_to(esend, ecore, c_sem.at[0], c_sem.at[1], (z, at(x, y, 1 - c)))
    core_copy.start()
    eown[...] = extras(c).reshape(16, 32, 1024).astype(BF16)
    core_copy.wait_recv()
    s1[...] = (eown[...].astype(F32) + ecore[...].astype(F32)).astype(BF16).reshape(4, 4, 32, 1024)

    left, right = pl.ds(0, 512), pl.ds(512, 512)

    def a2(k, into):
        to = lax.rem(x + k, SIDE)
        return copy_to(s1.at[to, :, :, left], r2a.at[into], x_send.at[0, into], x_recv.at[0, into], (z, at(to, y, c)))

    def b2(k, into):
        to = lax.rem(y + k, SIDE)
        return copy_to(s1.at[:, to, :, right], r2b.at[into], x_send.at[1, into], x_recv.at[1, into], (z, at(x, to, c)))

    def a3(k, into):
        to = lax.rem(y + k, SIDE)
        return copy_to(s2a.at[to], r3a.at[into], x_send.at[2, into], x_recv.at[2, into], (z, at(x, to, c)))

    def b3(k, into):
        to = lax.rem(x + k, SIDE)
        return copy_to(s2b.at[to], r3b.at[into], x_send.at[3, into], x_recv.at[3, into], (z, at(to, y, c)))

    for k in range(1, SIDE):
        a2(k, k - 1).start()
        b2(k, k - 1).start()
    for k in range(1, SIDE):
        a2(k, k - 1).wait_recv()
        b2(k, k - 1).wait_recv()

    def total(own, got):
        t = own.astype(F32)
        for k in range(SIDE - 1):
            t = t + got[k].astype(F32)
        return t.astype(BF16)

    s2a[...] = total(s1[x, :, :, 0:512], r2a)
    s2b[...] = total(s1[:, y, :, 512:1024], r2b)
    for k in range(1, SIDE):
        a3(k, k - 1).start()
        b3(k, k - 1).start()
    for k in range(1, SIDE):
        a3(k, k - 1).wait_recv()
        b3(k, k - 1).wait_recv()
    ext_ref[:, 0:512] = total(s2a[y], r3a)
    ext_ref[:, 512:1024] = total(s2b[x], r3b)

    each(lambda k: b_take(k).wait_recv())
    got = brecv[...].astype(F32)
    base_ref[:, 0:512] = got[:, 0:8].reshape(256, 512).astype(BF16)
    base_ref[:, 512:1024] = got[:, 8:16].reshape(256, 512).astype(BF16)
    table_ref[...] = in_buf[...].reshape(512, 128)
    each(lambda k: p_copy(k).wait_send())
    each(lambda k: b_copy(k).wait_send())
    core_copy.wait_send()
    for k in range(1, SIDE):
        for make in (a2, b2, a3, b3):
            make(k, k - 1).wait_send()


def fetch(pay, bank_emb):
    vm = pl.BlockSpec(memory_space=pltpu.VMEM)
    dma = pltpu.SemaphoreType.DMA
    return pl.pallas_call(
        fetch_kernel,
        out_shape=(
            jax.ShapeDtypeStruct((512, 128), F32),
            jax.ShapeDtypeStruct((288, 128), F32),
            jax.ShapeDtypeStruct((256, 1024), BF16),
            jax.ShapeDtypeStruct((32, 1024), BF16),
        ),
        in_specs=[vm, pl.BlockSpec(memory_space=pl.ANY)],
        out_specs=(vm,) * 4,
        scratch_shapes=[
            pltpu.VMEM((2048, 1024), BF16),
            pltpu.VMEM((32, 16, 128), F32),
            pltpu.VMEM((32, 16, 128), F32),
            pltpu.VMEM((32, 16, 512), BF16),
            pltpu.VMEM((32, 16, 512), BF16),
            pltpu.VMEM((16, 32, 1024), BF16),
            pltpu.VMEM((16, 32, 1024), BF16),
            pltpu.VMEM((16, 32, 1024), BF16),
            pltpu.VMEM((4, 4, 32, 1024), BF16),
            pltpu.VMEM((3, 4, 32, 512), BF16),
            pltpu.VMEM((3, 4, 32, 512), BF16),
            pltpu.VMEM((4, 32, 512), BF16),
            pltpu.VMEM((4, 32, 512), BF16),
            pltpu.VMEM((3, 32, 512), BF16),
            pltpu.VMEM((3, 32, 512), BF16),
            dma,
            dma((GROUP,)),
            dma((GROUP,)),
            dma((GROUP,)),
            dma((GROUP,)),
            dma((2,)),
            dma((4, 3)),
            dma((4, 3)),
        ],
        compiler_params=pltpu.CompilerParams(
            collective_id=0, has_side_effects=True, vmem_limit_bytes=56 * MIB
        ),
        name="fetch",
    )(pay, bank_emb)


def batcher(n):
    pairs = []
    p = 1
    while p < n:
        k = p
        while k >= 1:
            for j in range(k % p, n - k, 2 * k):
                for i in range(min(k, n - j - k)):
                    if (i + j) // (2 * p) == (i + j + k) // (2 * p):
                        pairs.append((i + j, i + j + k))
            k //= 2
        p *= 2
    return pairs


SORT16 = batcher(16)


def exchange(v, i, j):
    v[i], v[j] = jnp.minimum(v[i], v[j]), jnp.maximum(v[i], v[j])


def sort16(v):
    v = list(v)
    for i, j in SORT16:
        exchange(v, i, j)
    return v


def merge16(a, b):
    v = [jnp.minimum(a[i], b[15 - i]) for i in range(16)]
    for d in (8, 4, 2, 1):
        for i in range(16):
            if i & d == 0:
                exchange(v, i, i + d)
    return v


def sign_rows(table):
    hi = jnp.floor(table * (1.0 / 256.0))
    lo = table - 256.0 * hi
    both = jnp.concatenate([hi, lo], axis=1).astype(BF16)
    k = iota((1024, 256), 0)
    lane = iota((1024, 256), 1)
    source = (k >> 4) + jnp.where((k & 8) == 0, 128, 0)
    pick = jnp.where(lane == source, 1.0, 0.0).astype(BF16)
    byte = dot(pick, both, LAST).astype(jnp.int32)
    bit = byte & (1 << (iota((1024, 512), 0) & 7))
    signs = jnp.where(bit != 0, -1024.0, 1024.0).astype(BF16)
    lane16 = iota((16, 256), 1)
    weigh = jnp.where(lane16 == 64, 256.0, jnp.where(lane16 == 192, 1.0, 0.0)).astype(BF16)
    return signs, dot(weigh, both, LAST)


def search_kernel(table_ref, codes_hbm, best_ref, codes, signs, keys, pos, load_sem):
    me = lax.axis_index("index")
    load = pltpu.make_async_copy(codes_hbm, codes, load_sem)
    load.start()
    signs_v, pos_v = sign_rows(table_ref[...])
    signs[...] = signs_v
    pos[...] = pos_v[0:8] - (me * 2048).astype(F32)
    load.wait()

    def product(m, carry):
        at_row = pl.multiple_of(m * 256, 256)
        keys[pl.ds(at_row, 256), :] = dot(codes[pl.ds(at_row, 256), :], signs[...])
        return carry

    lax.fori_loop(0, 8, product, 0)
    sub = iota((8, 128), 0)
    for t in range(4):
        lanes = slice(t * 128, (t + 1) * 128)
        wanted = pos[:, lanes]

        def load16(g):
            out = []
            for i in range(16):
                row = pl.multiple_of(g * 128 + i * 8, 8)
                p = (sub + (g * 128 + i * 8)).astype(F32)
                key = keys[pl.ds(row, 8), lanes] + (p + float(1 << 20))
                out.append(jnp.where(p == wanted, BIG, key))
            return out

        def step(g, best):
            return tuple(merge16(best, sort16(load16(g))))

        best = lax.fori_loop(1, 16, step, tuple(sort16(load16(0))))
        for d in (4, 2, 1):
            best = merge16(best, [pltpu.roll(b, d, 0) for b in best])
        for i in range(16):
            best_ref[t, i : i + 1, :] = best[i][0:1, :]


def search(table, bank_codes):
    vm = pl.BlockSpec(memory_space=pltpu.VMEM)
    return pl.pallas_call(
        search_kernel,
        out_shape=jax.ShapeDtypeStruct((4, 16, 128), F32),
        in_specs=[vm, pl.BlockSpec(memory_space=pl.ANY)],
        out_specs=vm,
        scratch_shapes=[
            pltpu.VMEM((2048, 1024), BF16),
            pltpu.VMEM((1024, 512), BF16),
            pltpu.VMEM((2048, 512), F32),
            pltpu.VMEM((8, 512), F32),
            pltpu.SemaphoreType.DMA,
        ],
        compiler_params=pltpu.CompilerParams(vmem_limit_bytes=48 * MIB),
        name="search",
    )(table, bank_codes)


def split(v):
    high = v.astype(BF16)
    return high, (v - high.astype(F32)).astype(BF16)


def head_kernel(query_ref, positive_ref, base_ref, ext_ref, owned_ref, head_ref, qg_ref, pg_ref, send_ref, xs, dz):
    xs[0:16] = query_ref[...]
    xs[16:32] = positive_ref[...]
    xs[32:288] = base_ref[...]
    xs[288:320] = ext_ref[...]
    head = head_ref[...]
    zed = dot(xs[...], head)
    norm = jnp.sqrt(jnp.sum(zed * zed, axis=1, keepdims=True) + 1e-6)
    inv = 1.0 / norm
    unit = zed * inv
    q_hi, q_lo = split(unit[0:16])
    c_hi, c_lo = split(unit[16:320])
    cos = dot(c_hi, q_hi, LAST) + (dot(c_lo, q_hi, LAST) + dot(c_hi, q_lo, LAST))
    logits = 50.0 * cos
    own_pos = jnp.where(iota((16, 16), 0) == iota((16, 16), 1), 1.0, 0.0)
    mask = jnp.concatenate([own_pos, owned_ref[:, 0:16]], axis=0)
    weights = jnp.where(mask > 0.5, jnp.exp(jnp.where(mask > 0.5, logits, 0.0)), 0.0)
    probs = weights / jnp.sum(weights, axis=0, keepdims=True)
    slopes = probs - jnp.concatenate([own_pos, jnp.zeros((288, 16), F32)], axis=0)
    s_hi, s_lo = split(slopes)
    first_dims = (((0,), (0,)), ((), ()))
    du = 50.0 * (dot(s_hi, c_hi, first_dims) + (dot(s_lo, c_hi, first_dims) + dot(s_hi, c_lo, first_dims)))
    q_unit = unit[0:16]
    dz[0:16] = ((du - q_unit * jnp.sum(q_unit * du, axis=1, keepdims=True)) * inv[0:16]).astype(BF16)
    inv_c = inv[16:320]
    k1_hi, k1_lo = split(slopes * (50.0 * inv_c))
    k2 = jnp.sum(slopes * logits, axis=1, keepdims=True) * inv_c
    along = dot(k1_hi, q_hi) + (dot(k1_lo, q_hi) + dot(k1_hi, q_lo))
    dz[16:320] = (along - unit[16:320] * k2).astype(BF16)
    grads = dot(dz[0:32], head, LAST).astype(BF16)
    qg_ref[...] = grads[0:16]
    pg_ref[...] = grads[16:32]
    for m in range(8):
        part = dot(xs[:, m * 128 : (m + 1) * 128], dz[...], first_dims)
        part = part.reshape(16, 8, 1024)
        part = jnp.concatenate([part[:, :, 0:512], part[:, :, 512:1024]], axis=1).astype(BF16)
        part = part.reshape(2, 4, 2, 16, 512)
        x0 = (m % 2) * 2
        for core in range(2):
            send_ref[core, m // 2, x0 : x0 + 2] = part[:, :, core]


def head_backward(query_emb, positive_emb, base, ext, owned, head):
    vm = pl.BlockSpec(memory_space=pltpu.VMEM)
    return pl.pallas_call(
        head_kernel,
        out_shape=(
            jax.ShapeDtypeStruct((16, 1024), BF16),
            jax.ShapeDtypeStruct((16, 1024), BF16),
            jax.ShapeDtypeStruct((2, 4, 4, 4, 16, 512), BF16),
        ),
        in_specs=[vm] * 6,
        out_specs=(vm,) * 3,
        scratch_shapes=[pltpu.VMEM((320, 1024), BF16), pltpu.VMEM((320, 1024), BF16)],
        compiler_params=pltpu.CompilerParams(vmem_limit_bytes=48 * MIB),
        name="head",
    )(query_emb, positive_emb, base, ext, owned, head)


ORDERS = ((0, 1, 2), (1, 2, 0), (2, 0, 1), (0, 2, 1))


def finish_kernel(
    best_ref, send_ref, ids_ref, dist_ref, hg_ref,
    crecv, packed, square, core_in, parts, inbox, mids, inbox2, tail, inbox3,
    t_send, t_recv, c_sem, r_send, r_recv,
):
    z, me, x, y, c = coords()
    group_barrier(z, me, True)
    place = (z, x, y)

    def device(axis, to):
        where = [z, x, y]
        where[axis] = to
        return (where[0], at(where[1], where[2], c))

    core_copy = copy_to(send_ref.at[1 - c], core_in, c_sem.at[0], c_sem.at[1], (z, at(x, y, 1 - c)))
    core_copy.start()

    def t_copy(k):
        peer = lax.rem(me + k, GROUP)
        return copy_to(best_ref.at[lax.div(peer, 8)], crecv.at[me], t_send.at[peer], t_recv.at[me], (z, peer))

    def t_take(k):
        source = lax.rem(me + GROUP - k, GROUP)
        return copy_to(best_ref.at[0], crecv.at[source], t_send.at[source], t_recv.at[source], (z, source))

    def each(act):
        def step(k, carry):
            act(k)
            return carry

        lax.fori_loop(1, GROUP, step, 0)

    each(lambda k: t_copy(k).start())
    crecv[me] = best_ref[lax.div(me, 8)]

    core_copy.wait_recv()
    parts[...] = (send_ref[c].astype(F32) + core_in[...].astype(F32)).astype(BF16)

    def lanes(p):
        return pl.ds(p * 128, 128)

    def first(p, k):
        axis = ORDERS[p][0]
        to = lax.rem(place[axis] + k, SIDE)
        index = [slice(None)] * 3
        index[axis] = to
        return copy_to(
            parts.at[(*index, slice(None), lanes(p))], inbox.at[p, k - 1],
            r_send.at[0, p, k - 1], r_recv.at[0, p, k - 1], device(axis, to),
        )

    def second(p, k):
        axis = ORDERS[p][1]
        to = lax.rem(place[axis] + k, SIDE)
        rest = [a for a in range(3) if a != ORDERS[p][0]]
        index = [slice(None)] * 2
        index[rest.index(axis)] = to
        return copy_to(
            mids.at[(p, *index)], inbox2.at[p, k - 1],
            r_send.at[1, p, k - 1], r_recv.at[1, p, k - 1], device(axis, to),
        )

    def third(p, k):
        axis = ORDERS[p][2]
        to = lax.rem(place[axis] + k, SIDE)
        return copy_to(
            tail.at[p, to], inbox3.at[p, k - 1],
            r_send.at[2, p, k - 1], r_recv.at[2, p, k - 1], device(axis, to),
        )

    def total(own, got):
        t = own.astype(F32)
        for k in range(SIDE - 1):
            t = t + got[k].astype(F32)
        return t

    def start(make):
        for k in range(1, SIDE):
            for p in range(4):
                make(p, k).start()

    def arrive(make, p):
        for k in range(1, SIDE):
            make(p, k).wait_recv()

    start(first)

    each(lambda k: t_take(k).wait_recv())
    lane = iota((16, 128), 1)
    packed[...] = jnp.full((8, 16, 128), 2147483647, jnp.int32)
    mine = lax.rem(me, 8)
    for g in range(4):
        merged = jnp.zeros((16, 128), jnp.int32)
        for s in range(8):
            key = crecv[g * 8 + s].astype(jnp.int32)
            key = ((key >> 11) << 16) + (key & 2047) + (g * 8 + s) * 2048
            key = pltpu.roll(key, lax.rem((s - mine + 8) * 16, 128), 1)
            merged = jnp.where((lane >> 4) == s, key, merged)
        packed[g] = merged
    best = [packed[:, i, :] for i in range(16)]
    for d in (64, 32, 16):
        best = merge16(best, [pltpu.roll(b, d, 1) for b in best])
    for d in (6, 7):
        best = merge16(best, [pltpu.roll(b, d, 0) for b in best])
    for i in range(16):
        square[i : i + 1, :] = best[i][0:1, :]
    square[16:128, :] = jnp.zeros((112, 128), jnp.int32)
    flat = square[...]
    ids_ref[...] = jnp.transpose((flat & 65535).astype(F32))[0:16, 0:16].astype(jnp.int32)
    dist_ref[...] = jnp.transpose((flat >> 16).astype(F32))[0:16, 0:16].astype(jnp.int32)

    for p in range(4):
        arrive(first, p)
        index = [slice(None)] * 3
        index[ORDERS[p][0]] = place[ORDERS[p][0]]
        own = parts[(*index, slice(None), slice(p * 128, (p + 1) * 128))]
        mids[p] = total(own, inbox.at[p]).astype(BF16)
        for k in range(1, SIDE):
            second(p, k).start()
    for p in range(4):
        arrive(second, p)
        axis = ORDERS[p][1]
        rest = [a for a in range(3) if a != ORDERS[p][0]]
        index = [slice(None)] * 2
        index[rest.index(axis)] = place[axis]
        own = mids[(p, *index)]
        tail[p] = total(own, inbox2.at[p]).astype(BF16)
        for k in range(1, SIDE):
            third(p, k).start()
    for p in range(4):
        arrive(third, p)
        out = total(tail[p, place[ORDERS[p][2]]], inbox3.at[p])
        hg_ref[:, p * 128 : (p + 1) * 128] = out[0:8]
        hg_ref[:, 512 + p * 128 : 512 + (p + 1) * 128] = out[8:16]

    each(lambda k: t_copy(k).wait_send())
    core_copy.wait_send()
    for make in (first, second, third):
        for p in range(4):
            for k in range(1, SIDE):
                make(p, k).wait_send()


def finish(best, send):
    vm = pl.BlockSpec(memory_space=pltpu.VMEM)
    dma = pltpu.SemaphoreType.DMA
    return pl.pallas_call(
        finish_kernel,
        out_shape=(
            jax.ShapeDtypeStruct((16, 16), jnp.int32),
            jax.ShapeDtypeStruct((16, 16), jnp.int32),
            jax.ShapeDtypeStruct((8, 1024), F32),
        ),
        in_specs=[vm, vm],
        out_specs=(vm,) * 3,
        scratch_shapes=[
            pltpu.VMEM((32, 16, 128), F32),
            pltpu.VMEM((8, 16, 128), jnp.int32),
            pltpu.VMEM((128, 128), jnp.int32),
            pltpu.VMEM((4, 4, 4, 16, 512), BF16),
            pltpu.VMEM((4, 4, 4, 16, 512), BF16),
            pltpu.VMEM((4, 3, 4, 4, 16, 128), BF16),
            pltpu.VMEM((4, 4, 4, 16, 128), BF16),
            pltpu.VMEM((4, 3, 4, 16, 128), BF16),
            pltpu.VMEM((4, 4, 16, 128), BF16),
            pltpu.VMEM((4, 3, 16, 128), BF16),
            dma((GROUP,)),
            dma((GROUP,)),
            dma((2,)),
            dma((3, 4, 3)),
            dma((3, 4, 3)),
        ],
        compiler_params=pltpu.CompilerParams(
            collective_id=1, has_side_effects=True, vmem_limit_bytes=48 * MIB
        ),
        name="finish",
    )(best, send)


def local(
    query_codes, positive_ids, negative_ids, bank_codes, bank_emb, query_emb, positive_emb, head
):
    pay = jnp.concatenate([query_codes, positive_ids[:, None], negative_ids], axis=1).astype(F32)
    pay = jnp.pad(pay, ((0, 0), (0, 128 - pay.shape[1])))
    table, owned, base, ext = fetch(pay, bank_emb)
    best = search(table, bank_codes)
    query_grad, positive_grad, send = head_backward(query_emb, positive_emb, base, ext, owned, head)
    mined_ids, mined_dist, head_grad = finish(best, send)
    return (mined_ids, mined_dist, query_grad, positive_grad, head_grad)


def solution(mesh):
    both = ("dp", "index")
    rows = P(both, None)
    return jax.shard_map(
        local,
        mesh=mesh,
        in_specs=(rows, P(both), rows, P("index", None), P("index", None), rows, rows, P()),
        out_specs=(rows,) * 5,
        check_vma=False,
    )
```

time: 349 us -> 82.1 us (0.24); the launches traced: 343 us -> 81.2 us
  waiting for transfers between devices: 173 us -> 0 us
  Pallas kernels: 0 us -> 75.4 us
  other arithmetic: 45.8 us -> 0.94 us
  local copies, waits for them, and re-layouts: 45.8 us -> 4.18 us
  blocking collectives: 38.4 us -> 0 us
  matrix products: 17.6 us -> 0 us
  between operations: 16.3 us -> 0.74 us
  starting transfers between devices: 5.52 us -> 0 us
    psum x1 -> x0, waiting for transfers between devices: 146 us -> none  [local(): lax.psum(lax.dot_general(rows_all, slopes_all, (((0,), (0,)), ((), ())),...]
    pallas_call x0 -> x4, Pallas kernels: none -> 75.4 us  [the longest x1 38 us: fetch(): pl.pallas_call(fetch_kernel, out_shape=(jax.ShapeDtypeStruct((512, 128),...]
    reduce_min x33 -> x0, other arithmetic: 33.9 us -> none  [smallest_keys(): lowest = jnp.min(remaining, axis=1)]
    all_to_all x1 -> x0, waiting for transfers between devices: 27.5 us -> none  [local(): lax.all_to_all(fetched, 'index', split_axis=0, concat_axis=0, tiled=True)]
    all_gather x1 -> x0, blocking collectives: 26.5 us -> none  [local(): lax.all_gather(query_codes, 'index', axis=0, tiled=True)]
    dot_general x9 -> x0, matrix products: 17.6 us -> none  [the longest x1 5.22 us: local(): lax.dot_general(sign_bits, bank_codes, (((1,), (1,)), ((), ())), preferre...]
    gather x3 -> x0, local copies, waits for them, and re-layouts: 17 us -> none  [the longest x2 13.7 us: local(): fetched = jnp.take(bank_emb, asked_offsets.reshape(-1), axis=0)]
    scatter x1 -> x0, local copies, waits for them, and re-layouts: 12.7 us -> none  [local(): jnp.zeros((shards, capacity), jnp.int32).at[owner_of, position].set(offset)]
  transfers between devices with their start and end apart: 3 -> 0, of which waited for: 2 -> 0; matrix products, arithmetic and copies ran while one was open for 13% -> 0% of each run, Pallas kernels for 0% -> 0%
where the time goes in v1:
time: 82.1 us; the launch traced here: 81.2 us
  Pallas kernels  75.4 us (92%)
  local copies, waits for them, and re-layouts  4.18 us (5%)
  other arithmetic  0.94 us (1%)
    pallas_call x1, Pallas kernels, fetch(): pl.pallas_call(fetch_kernel, out_shape=(jax.ShapeDtypeStruct((512, 128),...  38 us
    pallas_call x1, Pallas kernels, finish(): pl.pallas_call(finish_kernel, out_shape=(jax.ShapeDtypeStruct((16, 16), j...  24.6 us
    pallas_call x1, Pallas kernels, search(): pl.pallas_call(search_kernel, out_shape=jax.ShapeDtypeStruct((4, 16, 128)...  7.58 us
    pallas_call x1, Pallas kernels, head_backward(): pl.pallas_call(head_kernel, out_shape=(jax.ShapeDtypeStruct((16, 1024), B...  5.22 us
    unnamed x19, local copies, waits for them, and re-layouts  2.84 us

profile of v1, /device:TPU:1, one launch (start us, length us, event | category | flops | bytes accessed | tf_op | source)
XLA Modules:
  0.0 81.2 jit_solution(17451661269071521176)
XLA Ops:
  0.6 0.7 copy.13
  1.4 0.0 copy-start
  1.4 0.9 %add_convert_fusion = f32[16,81]{1,0:T(8,128)S(1)} fusion(s32[16,16]{1,0:T(8,128)} %param.10, s32[16,1]{1,0:T(8,128)S(1)} %copy.13, s32[16,64]{1,0:T(8,128)} %param.8), kind=kLoop, calls=%fused_computation | loop fusion | flops 3888 | bytes 10368 | tf_op jit(solution)/shard_map/convert_element_type | solution.py:644
  2.3 0.6 pad.4.pay_ref
  2.9 0.0 copy-start.1
  2.9 38.0 %fetch.1 = (f32[512,128]{1,0:T(8,128)}, f32[288,128]{1,0:T(8,128)}, bf16[256,1024]{1,0:T(8,128)(2,1)}, bf16[32,1024]{1,0:T(8,128)(2,1)}) custom-call(f32[16,128]{1,0:T(8,128)} %pad.4.pay_ref, bf16[2048,1024]{1,0:T(8,128)(2,1)} %bank_hbm.1), custom_call_target="tpu_custom_call" | custom-call | tf_op jit(solution)/shard_map/fetch/pallas_call | solution.py:241
  40.9 0.0 copy-start.2
  40.9 0.0 copy-done
  40.9 0.0 copy-start.3
  41.0 1.0 %copy-done.3 = f32[512,128]{1,0:T(8,128)S(1)} copy-done((f32[512,128]{1,0:T(8,128)S(1)}, f32[512,128]{1,0:T(8,128)}, u32[]{:S(2)}) %copy-start.3) | copy-done | bytes 262168
  42.0 0.0 copy-start.4
  42.0 0.0 copy-start.5
  42.0 7.6 %search.1.best_ref = f32[4,16,128]{2,1,0:T(8,128)S(1)} custom-call(f32[512,128]{1,0:T(8,128)S(1)} %copy-done.3, bf16[2048,1024]{1,0:T(8,128)(2,1)S(1)} %copy-done), custom_call_target="tpu_custom_call" | custom-call | tf_op jit(solution)/shard_map/search/pallas_call | solution.py:378
  49.5 0.0 copy-done.1
  49.6 0.0 copy-done.2
  49.6 0.0 copy-done.4
  49.6 0.0 copy-done.5
  49.6 0.0 copy-done.6
  49.6 0.0 copy-done.7
  49.6 5.2 %head.1 = (bf16[16,1024]{1,0:T(8,128)(2,1)}, bf16[16,1024]{1,0:T(8,128)(2,1)}, bf16[2,4,4,4,16,512]{5,4,3,2,1,0:T(8,128)(2,1)S(1)}) custom-call(bf16[16,1024]{1,0:T(8,128)(2,1)S(1)} %copy-done.6, bf16[16,1024]{1,0:T(8,128)(2,1)S(1)} %copy-done.7, bf16[256,1024]{1,0:T(8,128)(2,1)S(1)} %copy-done.2, bf16[32,1024]{1,0:T(8,128)(2,1)S(1)} %copy-done.5, ...), custom_call_target="tpu_custom_call" | custom-call | tf_op jit(solution)/shard_map/head/pallas_call | solution.py:444
  54.8 24.6 %finish.1 = (s32[16,16]{1,0:T(8,128)S(1)}, s32[16,16]{1,0:T(8,128)S(1)}, f32[8,1024]{1,0:T(8,128)S(1)}) custom-call(f32[4,16,128]{2,1,0:T(8,128)S(1)} %search.1.best_ref, bf16[2,4,4,4,16,512]{5,4,3,2,1,0:T(8,128)(2,1)S(1)} %get-tuple-element.19.send_ref), custom_call_target="tpu_custom_call" | custom-call | tf_op jit(solution)/shard_map/finish/pallas_call | solution.py:608
  79.4 0.6 copy.17
  80.0 0.6 copy.18
  80.6 0.6 copy.19
  (2 shorter events, 0.0 us)
Async XLA Ops:
  1.4 39.6 %copy-start = (bf16[2048,1024]{1,0:T(8,128)(2,1)S(1)}, bf16[2048,1024]{1,0:T(8,128)(2,1)}, u32[]{:S(2)}) copy-start(bf16[2048,1024]{1,0:T(8,128)(2,1)} %codes_hbm.1) | copy-start | bytes 12582916
  2.9 46.6 %copy-start.1 = (bf16[1024,1024]{1,0:T(8,128)(2,1)S(1)}, bf16[1024,1024]{1,0:T(8,128)(2,1)}, u32[]{:S(2)}) copy-start(bf16[1024,1024]{1,0:T(8,128)(2,1)} %head_ref.1) | copy-start | bytes 6291460
  40.9 8.6 %copy-start.2 = (bf16[256,1024]{1,0:T(8,128)(2,1)S(1)}, bf16[256,1024]{1,0:T(8,128)(2,1)}, u32[]{:S(2)}) copy-start(bf16[256,1024]{1,0:T(8,128)(2,1)} %get-tuple-element.16.base_ref) | copy-start | bytes 1572868
  40.9 1.0 %copy-start.3 = (f32[512,128]{1,0:T(8,128)S(1)}, f32[512,128]{1,0:T(8,128)}, u32[]{:S(2)}) copy-start(f32[512,128]{1,0:T(8,128)} %get-tuple-element.15.table_ref) | copy-start | bytes 786436
  42.0 7.6 %copy-start.4 = (f32[288,128]{1,0:T(8,128)S(1)}, f32[288,128]{1,0:T(8,128)}, u32[]{:S(2)}) copy-start(f32[288,128]{1,0:T(8,128)} %get-tuple-element.18.owned_ref) | copy-start | bytes 442372
  42.0 7.6 %copy-start.5 = (bf16[32,1024]{1,0:T(8,128)(2,1)S(1)}, bf16[32,1024]{1,0:T(8,128)(2,1)}, u32[]{:S(2)}) copy-start(bf16[32,1024]{1,0:T(8,128)(2,1)} %get-tuple-element.17.ext_ref) | copy-start | bytes 196612
  42.0 7.6 %copy-start.6 = (bf16[16,1024]{1,0:T(8,128)(2,1)S(1)}, bf16[16,1024]{1,0:T(8,128)(2,1)}, u32[]{:S(2)}) copy-start(bf16[16,1024]{1,0:T(8,128)(2,1)} %query_ref.1) | copy-start | bytes 98308
  42.0 7.6 %copy-start.7 = (bf16[16,1024]{1,0:T(8,128)(2,1)S(1)}, bf16[16,1024]{1,0:T(8,128)(2,1)}, u32[]{:S(2)}) copy-start(bf16[16,1024]{1,0:T(8,128)(2,1)} %positive_ref.1) | copy-start | bytes 98308

commit v2 on v0

v2 whole, which is shorter than its diff:
```python
import functools

import jax
import jax.numpy as jnp
from jax import lax
from jax.experimental import pallas as pl
from jax.experimental.pallas import tpu as pltpu
from jax.sharding import PartitionSpec as P

F32 = jnp.float32
BF16 = jnp.bfloat16
MESH = pl.DeviceIdType.MESH
MIB = 1 << 20
GROUP = 32
SIDE = 4
BIG = float(1 << 23)
LAST = (((1,), (1,)), ((), ()))


def iota(shape, dim):
    return lax.broadcasted_iota(jnp.int32, shape, dim)


def dot(a, b, dims=(((1,), (0,)), ((), ()))):
    return lax.dot_general(a, b, dims, preferred_element_type=F32)


def copy_to(src, dst, send_sem, recv_sem, device):
    return pltpu.make_async_remote_copy(
        src_ref=src,
        dst_ref=dst,
        send_sem=send_sem,
        recv_sem=recv_sem,
        device_id=device,
        device_id_type=MESH,
    )


def coords():
    z = lax.axis_index("dp")
    me = lax.axis_index("index")
    x = lax.div(me, 8)
    y = lax.rem(lax.div(me, 2), 4)
    c = lax.rem(me, 2)
    return z, me, x, y, c


def at(x, y, c):
    return x * 8 + y * 2 + c


OFFSETS = sorted(
    ((dx, dy, dc) for dx in range(4) for dy in range(4) for dc in range(2) if dx or dy or dc),
    key=lambda o: -(min(o[0], 4 - o[0]) + min(o[1], 4 - o[1])),
)


def peers(x, y, c):
    return [at(lax.rem(x + dx, 4), lax.rem(y + dy, 4), lax.rem(c + dc, 2)) for dx, dy, dc in OFFSETS]


def take(ref, sem):
    pltpu.make_async_copy(ref, ref, sem).wait()


def request_table(codes, pos_row, negatives):
    hi = jnp.floor(negatives * (1.0 / 256.0))
    lo = negatives - 256.0 * hi
    halves = jnp.concatenate([hi, lo], axis=0).astype(BF16)
    spread = jnp.where(iota((16, 256), 0) == (iota((16, 256), 1) & 15), 1.0, 0.0).astype(BF16)
    got = dot(halves, spread)
    ids = 256.0 * got[0:16] + got[16:32]
    ids = jnp.where(iota((16, 256), 0) == (iota((16, 256), 1) >> 4), ids, 0.0)
    id_row = jnp.sum(ids, axis=0, keepdims=True)
    owner_row = jnp.floor(id_row * (1.0 / 2048.0))
    owner_b = jnp.broadcast_to(owner_row, (256, 256))
    owner_t = jnp.transpose(owner_b)
    earlier = iota((256, 256), 0) < iota((256, 256), 1)
    same = jnp.where(owner_b == owner_t, 1.0, 0.0)
    rank = jnp.sum(jnp.where(earlier, same, 0.0), axis=0, keepdims=True)
    slot_row = jnp.where(rank < 7.0, owner_row * 8.0 + rank, 249.0 + rank)
    slot_b = jnp.broadcast_to(slot_row, (288, 256))
    hit = iota((288, 256), 0).astype(F32) == slot_b
    id_col = jnp.sum(jnp.where(hit, jnp.broadcast_to(id_row, (288, 256)) + 1.0, 0.0), axis=1, keepdims=True) - 1.0
    which = jnp.where(iota((256, 128), 1) == (iota((256, 128), 0) >> 4), 1.0, 0.0).astype(BF16)
    owned_by = dot(jnp.where(hit, 1.0, 0.0).astype(BF16), which)
    lane32 = iota((32, 128), 1)
    sub32 = iota((32, 128), 0)
    ext_row = jnp.sum(
        jnp.where(lane32 == sub32 + 96, jnp.broadcast_to(id_col[256:288], (32, 128)), 0.0), axis=0, keepdims=True
    )
    diagonal = iota((16, 16), 0) == iota((16, 16), 1)
    pos_col = jnp.sum(jnp.where(diagonal, jnp.broadcast_to(pos_row, (16, 16)), 0.0), axis=1, keepdims=True)
    lane16 = iota((16, 128), 1)
    rest = jnp.where(lane16 >= 96, jnp.broadcast_to(ext_row, (16, 128)), 0.0)
    rest = jnp.where(lane16 == 64, jnp.broadcast_to(pos_col, (16, 128)), rest)
    return id_col, owned_by, jnp.where(lane16 < 64, codes, rest)


def onehot_rows(rel, count):
    return jnp.where(
        jnp.broadcast_to(rel, (count, 2048)) == iota((count, 2048), 1).astype(F32), 1.0, 0.0
    ).astype(BF16)


def batcher(n):
    pairs = []
    p = 1
    while p < n:
        k = p
        while k >= 1:
            for j in range(k % p, n - k, 2 * k):
                for i in range(min(k, n - j - k)):
                    if (i + j) // (2 * p) == (i + j + k) // (2 * p):
                        pairs.append((i + j, i + j + k))
            k //= 2
        p *= 2
    return pairs


SORT16 = batcher(16)


def exchange(v, i, j):
    v[i], v[j] = jnp.minimum(v[i], v[j]), jnp.maximum(v[i], v[j])


def sort16(v):
    v = list(v)
    for i, j in SORT16:
        exchange(v, i, j)
    return v


def merge16(a, b):
    v = [jnp.minimum(a[i], b[15 - i]) for i in range(16)]
    for d in (8, 4, 2, 1):
        for i in range(16):
            if i & d == 0:
                exchange(v, i, i + d)
    return v


def sign_rows(table):
    hi = jnp.floor(table * (1.0 / 256.0))
    lo = table - 256.0 * hi
    both = jnp.concatenate([hi, lo], axis=1).astype(BF16)
    k = iota((1024, 256), 0)
    lane = iota((1024, 256), 1)
    source = (k >> 4) + jnp.where((k & 8) == 0, 128, 0)
    pick = jnp.where(lane == source, 1.0, 0.0).astype(BF16)
    byte = dot(pick, both, LAST).astype(jnp.int32)
    bit = byte & (1 << (iota((1024, 512), 0) & 7))
    signs = jnp.where(bit != 0, -1024.0, 1024.0).astype(BF16)
    lane16 = iota((16, 256), 1)
    weigh = jnp.where(lane16 == 64, 256.0, jnp.where(lane16 == 192, 1.0, 0.0)).astype(BF16)
    return signs, dot(weigh, both, LAST)


PORTIONS = ((0, 0, 4, (0, 1, 2)), (1, 0, 4, (1, 2, 0)), (2, 0, 4, (2, 0, 1)), (3, 0, 2, (0, 1, 2)), (3, 2, 2, (1, 0, 2)))
TAIL = (0, 1, 2, 3, 3)


def extents(p, stage):
    _, _, ys, order = PORTIONS[p]
    return [(a, ys if a == 2 else SIDE) for a in range(3) if a not in order[:stage]]


def split(v):
    high = v.astype(BF16)
    return high, (v - high.astype(F32)).astype(BF16)


def whole_kernel(
    qcodes_ref, pos_ref, neg_ref, codes_hbm, bank_hbm, query_ref, positive_ref, head_hbm,
    best_ref, grads_ref, hg_ref,
    bank, codes, head, pay, owned, out_buf, in_buf, bsend, brecv, esend, eown, ecore, s1, r2a, r2b, s2a, s2b, r3a, r3b,
    signs, keys, pos, shard_best, crecv, packed, xs, dz, unit, inv, u_hi, u_lo,
    hs, core_in, parts, in1, mid, in2, tail, in3,
    load_sem, p_sem, b_sem, t_sem, c_sem, x_send, x_recv, h_send, h_recv, r_send, r_recv,
):
    z, me, x, y, c = coords()
    others = peers(x, y, c)
    partner = (z, at(x, y, 1 - c))
    load_bank = pltpu.make_async_copy(bank_hbm, bank, load_sem.at[0])
    load_codes = pltpu.make_async_copy(codes_hbm, codes, load_sem.at[1])
    load_head = pltpu.make_async_copy(head_hbm, head, load_sem.at[2])
    load_bank.start()
    barrier = pltpu.get_barrier_semaphore()
    for peer in others:
        pl.semaphore_signal(barrier, inc=1, device_id=(z, peer), device_id_type=MESH)
    for k in range(1, SIDE):
        pl.semaphore_signal(barrier, inc=1, device_id=(lax.rem(z + k, SIDE), me), device_id_type=MESH)
    load_codes.start()
    load_head.start()

    pay[...] = jnp.zeros((16, 128), F32)
    pay[:, 0:64] = qcodes_ref[...].astype(F32)
    id_col, owned_by, common = request_table(pay[...], pos_ref[...].astype(F32), neg_ref[...].astype(F32))
    owned[...] = owned_by
    lane = iota((32, 8, 128), 2)
    base_cols = jnp.broadcast_to(id_col[0:256], (256, 128)).reshape(32, 8, 128)
    out_buf[:, 0:8, :] = jnp.where(lane == 65, base_cols, jnp.broadcast_to(common[None, 0:8], (32, 8, 128)))
    out_buf[:, 8:16, :] = jnp.broadcast_to(common[None, 8:16], (32, 8, 128))
    pl.semaphore_wait(barrier, len(others) + SIDE - 1)
    for peer in others:
        copy_to(out_buf.at[peer], in_buf.at[me], p_sem.at[0], p_sem.at[1], (z, peer)).start()
    in_buf[me] = out_buf[me]

    xs[0:16] = query_ref[...]
    xs[16:32] = positive_ref[...]

    def project(start, count):
        rows = slice(start, start + count)
        zed = dot(xs[rows], head[...])
        scale = 1.0 / jnp.sqrt(jnp.sum(zed * zed, axis=1, keepdims=True) + 1e-6)
        u = zed * scale
        unit[rows] = u
        inv[rows] = jnp.broadcast_to(scale, (count, 128))
        high, low = split(u)
        u_hi[rows] = high
        u_lo[rows] = low

    load_head.wait()
    project(0, 32)
    load_bank.wait()
    take(in_buf.at[pl.ds(0, GROUP - 1)], p_sem.at[1])

    first = (me * 2048).astype(F32)
    asked = in_buf[:, 0:8, :].reshape(256, 128)
    base_rel = jnp.sum(jnp.where(iota((256, 128), 1) == 65, asked, 0.0), axis=1, keepdims=True) - first
    hot = onehot_rows(base_rel, 256)
    for h in range(2):
        part = dot(hot, bank[:, h * 512 : (h + 1) * 512])
        bsend[:, 8 * h : 8 * h + 8, :] = part.reshape(32, 8, 512).astype(BF16)
    for peer in others:
        copy_to(bsend.at[peer], brecv.at[me], b_sem.at[0], b_sem.at[1], (z, peer)).start()
    brecv[me] = bsend[me]

    def extras(core):
        rows = in_buf[:, 0:1, :].reshape(16, 2, 1, 128)
        mine = jnp.where(core == 0, rows[:, 0], rows[:, 1])
        wide = jnp.broadcast_to(mine, (16, 32, 128))
        keep = iota((16, 32, 128), 2) == iota((16, 32, 128), 1) + 96
        rel = jnp.sum(jnp.where(keep, wide, 0.0), axis=2, keepdims=True).reshape(512, 1) - first
        return dot(onehot_rows(rel, 512), bank[...])

    esend[...] = extras(1 - c).reshape(16, 32, 1024).astype(BF16)
    core_copy = copy_to(esend, ecore, c_sem.at[0], c_sem.at[1], partner)
    core_copy.start()
    eown[...] = extras(c).reshape(16, 32, 1024).astype(BF16)
    core_copy.wait_recv()
    s1[...] = (eown[...].astype(F32) + ecore[...].astype(F32)).astype(BF16).reshape(4, 4, 32, 1024)

    left, right = pl.ds(0, 512), pl.ds(512, 512)
    for k in (2, 1, 3):
        to = lax.rem(x + k, SIDE)
        copy_to(s1.at[to, :, :, left], r2a.at[k - 1], x_send.at[0], x_recv.at[0], (z, at(to, y, c))).start()
        to = lax.rem(y + k, SIDE)
        copy_to(s1.at[:, to, :, right], r2b.at[k - 1], x_send.at[1], x_recv.at[1], (z, at(x, to, c))).start()

    signs_v, pos_v = sign_rows(in_buf[...].reshape(512, 128))
    signs[...] = signs_v
    pos[...] = pos_v[0:8] - first
    load_codes.wait()

    def product(m, carry):
        at_row = pl.multiple_of(m * 256, 256)
        keys[pl.ds(at_row, 256), :] = dot(codes[pl.ds(at_row, 256), :], signs[...])
        return carry

    lax.fori_loop(0, 8, product, 0)
    sub = iota((8, 128), 0)

    def select(t):
        lanes = slice(t * 128, (t + 1) * 128)
        wanted = pos[:, lanes]

        def load16(g):
            out = []
            for i in range(16):
                row = pl.multiple_of(g * 128 + i * 8, 8)
                p = (sub + (g * 128 + i * 8)).astype(F32)
                key = keys[pl.ds(row, 8), lanes] + (p + float(1 << 20))
                out.append(jnp.where(p == wanted, BIG, key))
            return out

        def step(g, best):
            return tuple(merge16(best, sort16(load16(g))))

        best = lax.fori_loop(1, 16, step, tuple(sort16(load16(0))))
        for d in (4, 2, 1):
            best = merge16(best, [pltpu.roll(b, d, 0) for b in best])
        for i in range(16):
            shard_best[t, i : i + 1, :] = best[i][0:1, :]

    select(0)
    select(1)

    def total(own, got):
        t = own.astype(F32)
        for k in range(SIDE - 1):
            t = t + got[k].astype(F32)
        return t

    take(r2a, x_recv.at[0])
    take(r2b, x_recv.at[1])
    s2a[...] = total(s1[x, :, :, 0:512], r2a).astype(BF16)
    s2b[...] = total(s1[:, y, :, 512:1024], r2b).astype(BF16)
    for k in (2, 1, 3):
        to = lax.rem(y + k, SIDE)
        copy_to(s2a.at[to], r3a.at[k - 1], x_send.at[2], x_recv.at[2], (z, at(x, to, c))).start()
        to = lax.rem(x + k, SIDE)
        copy_to(s2b.at[to], r3b.at[k - 1], x_send.at[3], x_recv.at[3], (z, at(to, y, c))).start()

    select(2)
    select(3)
    for peer in others:
        copy_to(shard_best.at[lax.div(peer, 8)], crecv.at[me], t_sem.at[0], t_sem.at[1], (z, peer)).start()
    crecv[me] = shard_best[lax.div(me, 8)]

    take(brecv.at[pl.ds(0, GROUP - 1)], b_sem.at[1])
    got = brecv[...].astype(F32)
    xs[32:288, 0:512] = got[:, 0:8].reshape(256, 512).astype(BF16)
    xs[32:288, 512:1024] = got[:, 8:16].reshape(256, 512).astype(BF16)
    project(32, 256)
    take(r3a, x_recv.at[2])
    take(r3b, x_recv.at[3])
    xs[288:320, 0:512] = total(s2a[y], r3a).astype(BF16)
    xs[288:320, 512:1024] = total(s2b[x], r3b).astype(BF16)
    project(288, 32)

    q_hi, q_lo = u_hi[0:16], u_lo[0:16]
    c_hi, c_lo = u_hi[16:320], u_lo[16:320]
    logits = 50.0 * (dot(c_hi, q_hi, LAST) + (dot(c_lo, q_hi, LAST) + dot(c_hi, q_lo, LAST)))
    own_pos = jnp.where(iota((16, 16), 0) == iota((16, 16), 1), 1.0, 0.0)
    mask = jnp.concatenate([own_pos, owned[:, 0:16]], axis=0)
    weights = jnp.where(mask > 0.5, jnp.exp(jnp.where(mask > 0.5, logits, 0.0)), 0.0)
    probs = weights / jnp.sum(weights, axis=0, keepdims=True)
    slopes = probs - jnp.concatenate([own_pos, jnp.zeros((288, 16), F32)], axis=0)
    s_hi, s_lo = split(slopes)
    firsts = (((0,), (0,)), ((), ()))
    du = 50.0 * (dot(s_hi, c_hi, firsts) + (dot(s_lo, c_hi, firsts) + dot(s_hi, c_lo, firsts)))
    q_unit = unit[0:16]
    dz[0:16] = ((du - q_unit * jnp.sum(q_unit * du, axis=1, keepdims=True)) * inv[0:16, 0:1]).astype(BF16)
    inv_c = inv[16:320, 0:1]
    k1_hi, k1_lo = split(slopes * (50.0 * inv_c))
    k2 = jnp.sum(slopes * logits, axis=1, keepdims=True) * inv_c
    along = dot(k1_hi, q_hi) + (dot(k1_lo, q_hi) + dot(k1_hi, q_lo))
    dz[16:320] = (along - unit[16:320] * k2).astype(BF16)

    def piece(i):
        m = lax.rem(2 * (z + 1) + i, 8)
        return m, lax.div(m, 2), pl.ds(lax.rem(m, 2) * 2, 2)

    def h_copy(i):
        m, zz, xx = piece(i)
        return copy_to(hs.at[1 - c, zz, xx], core_in.at[zz, xx], h_send, h_recv.at[m], partner)

    def grow(i, carry):
        m, zz, xx = piece(i)
        part = dot(xs[:, pl.ds(pl.multiple_of(m * 128, 128), 128)], dz[...], firsts).reshape(16, 8, 1024)
        part = jnp.concatenate([part[:, :, 0:512], part[:, :, 512:1024]], axis=1).astype(BF16)
        part = part.reshape(2, 4, 2, 16, 512)
        for core in range(2):
            hs[core, zz, xx] = part[:, :, core]
        h_copy(i).start()
        return carry

    lax.fori_loop(0, 8, grow, 0)

    place = (z, x, y)

    def device(axis, to):
        where = [z, x, y]
        where[axis] = to
        return (where[0], at(where[1], where[2], c))

    def first_from(p, to):
        tile, y0, ys, order = PORTIONS[p]
        index = [slice(None), slice(None), pl.ds(y0, ys)]
        if order[0] == 2:
            index[2] = to
        else:
            index[order[0]] = to
        return (*index, slice(None), pl.ds(tile * 128, 128))

    def send_first(p, k):
        axis = PORTIONS[p][3][0]
        to = lax.rem(place[axis] + k, SIDE)
        copy_to(
            parts.at[first_from(p, to)], in1[p].at[k - 1], r_send.at[0, p], r_recv.at[0, p], device(axis, to)
        ).start()

    for i in range(8):
        m, zz, xx = piece(i)
        h_copy(i).wait_recv()
        parts[zz, xx] = (hs[c, zz, xx].astype(F32) + core_in[zz, xx].astype(F32)).astype(BF16)
        if i % 2 == 1 and i < 6:
            send_first(0, i // 2 + 1)
            send_first(3, i // 2 + 1)
    for k in (2, 1, 3):
        for p in (1, 4, 2):
            send_first(p, k)

    grads_ref[...] = dot(dz[0:32], head[...], LAST).astype(BF16)

    take(crecv.at[pl.ds(0, GROUP - 1)], t_sem.at[1])
    lane = iota((16, 128), 1)
    packed[...] = jnp.full((8, 16, 128), 2147483647, jnp.int32)
    mine = lax.rem(me, 8)
    for g in range(4):
        merged = jnp.zeros((16, 128), jnp.int32)
        for s in range(8):
            key = crecv[g * 8 + s].astype(jnp.int32)
            key = ((key >> 11) << 16) + (key & 2047) + (g * 8 + s) * 2048
            key = pltpu.roll(key, lax.rem((s - mine + 8) * 16, 128), 1)
            merged = jnp.where((lane >> 4) == s, key, merged)
        packed[g] = merged
    best = [packed[:, i, :] for i in range(16)]
    for d in (64, 32, 16):
        best = merge16(best, [pltpu.roll(b, d, 1) for b in best])
    for d in (6, 7):
        best = merge16(best, [pltpu.roll(b, d, 0) for b in best])
    for i in range(16):
        best_ref[i : i + 1, :] = best[i][0:1, :]

    def pick(p, stage, to):
        axis = PORTIONS[p][3][stage]
        return tuple(to if a == axis else slice(None) for a, _ in extents(p, stage))

    for p in (1, 2, 4, 0, 3):
        axis = PORTIONS[p][3][0]
        take(in1[p], r_recv.at[0, p])
        mid[p][...] = total(parts[first_from(p, place[axis])], in1[p]).astype(BF16)
        axis = PORTIONS[p][3][1]
        for k in (2, 1, 3):
            to = lax.rem(place[axis] + k, SIDE)
            copy_to(
                mid[p].at[pick(p, 1, to)], in2[p].at[k - 1], r_send.at[1, p], r_recv.at[1, p], device(axis, to)
            ).start()
    for p in (1, 2, 4, 0, 3):
        axis = PORTIONS[p][3][1]
        take(in2[p], r_recv.at[1, p])
        _, y0, ys, order = PORTIONS[p]
        sums = total(mid[p][pick(p, 1, place[axis])], in2[p]).astype(BF16)
        if TAIL[p] == 3:
            tail[3, y0 : y0 + ys] = sums
        else:
            tail[p] = sums
        if p == 4:
            continue
        q = TAIL[p]
        axis = order[2]
        for k in (2, 1, 3):
            to = lax.rem(place[axis] + k, SIDE)
            copy_to(
                tail.at[q, to], in3.at[q, k - 1], r_send.at[2, q], r_recv.at[2, q], device(axis, to)
            ).start()
    for q in range(4):
        take(in3.at[q], r_recv.at[2, q])
        out = total(tail[q, place[PORTIONS[q][3][2]]], in3.at[q])
        hg_ref[:, q * 128 : (q + 1) * 128] = out[0:8]
        hg_ref[:, 512 + q * 128 : 512 + (q + 1) * 128] = out[8:16]

    take(out_buf.at[pl.ds(0, GROUP - 1)], p_sem.at[0])
    take(bsend.at[pl.ds(0, GROUP - 1)], b_sem.at[0])
    take(crecv.at[pl.ds(0, GROUP - 1)], t_sem.at[0])
    core_copy.wait_send()
    take(r2a, x_send.at[0])
    take(r2b, x_send.at[1])
    take(r3a, x_send.at[2])
    take(r3b, x_send.at[3])
    take(core_in, h_send)
    for p in range(5):
        take(in1[p], r_send.at[0, p])
        take(in2[p], r_send.at[1, p])
    for q in range(4):
        take(in3.at[q], r_send.at[2, q])


def whole(codes, pos, neg, bank_codes, bank_emb, query_emb, positive_emb, head):
    vm = pl.BlockSpec(memory_space=pltpu.VMEM)
    anywhere = pl.BlockSpec(memory_space=pl.ANY)
    dma = pltpu.SemaphoreType.DMA
    block = (16, 128)

    def by_portion(stage, lead):
        return [pltpu.VMEM((*lead, *(n for _, n in extents(p, stage)), *block), BF16) for p in range(5)]

    return pl.pallas_call(
        whole_kernel,
        out_shape=(
            jax.ShapeDtypeStruct((16, 128), jnp.int32),
            jax.ShapeDtypeStruct((32, 1024), BF16),
            jax.ShapeDtypeStruct((8, 1024), F32),
        ),
        in_specs=[vm, vm, vm, anywhere, anywhere, vm, vm, anywhere],
        out_specs=(vm,) * 3,
        scratch_shapes=[
            pltpu.VMEM((2048, 1024), BF16),
            pltpu.VMEM((2048, 1024), BF16),
            pltpu.VMEM((1024, 1024), BF16),
            pltpu.VMEM((16, 128), F32),
            pltpu.VMEM((288, 128), F32),
            pltpu.VMEM((32, 16, 128), F32),
            pltpu.VMEM((32, 16, 128), F32),
            pltpu.VMEM((32, 16, 512), BF16),
            pltpu.VMEM((32, 16, 512), BF16),
            pltpu.VMEM((16, 32, 1024), BF16),
            pltpu.VMEM((16, 32, 1024), BF16),
            pltpu.VMEM((16, 32, 1024), BF16),
            pltpu.VMEM((4, 4, 32, 1024), BF16),
            pltpu.VMEM((3, 4, 32, 512), BF16),
            pltpu.VMEM((3, 4, 32, 512), BF16),
            pltpu.VMEM((4, 32, 512), BF16),
            pltpu.VMEM((4, 32, 512), BF16),
            pltpu.VMEM((3, 32, 512), BF16),
            pltpu.VMEM((3, 32, 512), BF16),
            pltpu.VMEM((1024, 512), BF16),
            pltpu.VMEM((2048, 512), F32),
            pltpu.VMEM((8, 512), F32),
            pltpu.VMEM((4, 16, 128), F32),
            pltpu.VMEM((32, 16, 128), F32),
            pltpu.VMEM((8, 16, 128), jnp.int32),
            pltpu.VMEM((320, 1024), BF16),
            pltpu.VMEM((320, 1024), BF16),
            pltpu.VMEM((320, 1024), F32),
            pltpu.VMEM((320, 128), F32),
            pltpu.VMEM((320, 1024), BF16),
            pltpu.VMEM((320, 1024), BF16),
            pltpu.VMEM((2, 4, 4, 4, 16, 512), BF16),
            pltpu.VMEM((4, 4, 4, 16, 512), BF16),
            pltpu.VMEM((4, 4, 4, 16, 512), BF16),
            by_portion(1, (3,)),
            by_portion(1, ()),
            by_portion(2, (3,)),
            pltpu.VMEM((4, 4, *block), BF16),
            pltpu.VMEM((4, 3, *block), BF16),
            dma((3,)),
            dma((2,)),
            dma((2,)),
            dma((2,)),
            dma((2,)),
            dma((4,)),
            dma((4,)),
            dma,
            dma((8,)),
            dma((3, 5)),
            dma((3, 5)),
        ],
        compiler_params=pltpu.CompilerParams(
            collective_id=0, has_side_effects=True, vmem_limit_bytes=60 * MIB
        ),
        name="whole",
    )(codes, pos, neg, bank_codes, bank_emb, query_emb, positive_emb, head)


def emit_kernel(best_ref, grads_ref, sums_ref, ids_ref, dist_ref, qg_ref, pg_ref, hg_ref, square):
    square[...] = jnp.zeros((128, 128), jnp.int32)
    square[0:16, :] = best_ref[...]
    flat = square[...]
    ids_ref[...] = jnp.transpose((flat & 65535).astype(F32))[0:16, 0:16].astype(jnp.int32)
    dist_ref[...] = jnp.transpose((flat >> 16).astype(F32))[0:16, 0:16].astype(jnp.int32)
    qg_ref[...] = grads_ref[0:16]
    pg_ref[...] = grads_ref[16:32]
    hg_ref[...] = sums_ref[...]


def emit(best, grads, sums):
    vm = pl.BlockSpec(memory_space=pltpu.VMEM)
    return pl.pallas_call(
        emit_kernel,
        out_shape=(
            jax.ShapeDtypeStruct((16, 16), jnp.int32),
            jax.ShapeDtypeStruct((16, 16), jnp.int32),
            jax.ShapeDtypeStruct((16, 1024), BF16),
            jax.ShapeDtypeStruct((16, 1024), BF16),
            jax.ShapeDtypeStruct((8, 1024), F32),
        ),
        in_specs=[vm] * 3,
        out_specs=(vm,) * 5,
        scratch_shapes=[pltpu.VMEM((128, 128), jnp.int32)],
        name="emit",
    )(best, grads, sums)


def local(
    query_codes, positive_ids, negative_ids, bank_codes, bank_emb, query_emb, positive_emb, head
):
    return emit(
        *whole(
            query_codes, positive_ids.reshape(1, -1), negative_ids, bank_codes, bank_emb, query_emb, positive_emb, head
        )
    )


def solution(mesh):
    both = ("dp", "index")
    rows = P(both, None)
    return jax.shard_map(
        local,
        mesh=mesh,
        in_specs=(rows, P(both), rows, P("index", None), P("index", None), rows, rows, P()),
        out_specs=(rows,) * 5,
        check_vma=False,
    )
```

time: 349 us -> 57.8 us (0.17); the launches traced: 343 us -> 57.6 us
  waiting for transfers between devices: 173 us -> 0 us
  Pallas kernels: 0 us -> 56.9 us
  other arithmetic: 45.8 us -> 0 us
  local copies, waits for them, and re-layouts: 45.8 us -> 0 us
  blocking collectives: 38.4 us -> 0 us
  matrix products: 17.6 us -> 0 us
  between operations: 16.3 us -> 0.64 us
  starting transfers between devices: 5.52 us -> 0 us
    psum x1 -> x0, waiting for transfers between devices: 146 us -> none  [local(): lax.psum(lax.dot_general(rows_all, slopes_all, (((0,), (0,)), ((), ())),...]
    pallas_call x0 -> x2, Pallas kernels: none -> 56.9 us  [the longest x1 55.4 us: whole(): pl.pallas_call(whole_kernel, out_shape=(jax.ShapeDtypeStruct((16, 128), j...]
    reduce_min x33 -> x0, other arithmetic: 33.9 us -> none  [smallest_keys(): lowest = jnp.min(remaining, axis=1)]
    all_to_all x1 -> x0, waiting for transfers between devices: 27.5 us -> none  [local(): lax.all_to_all(fetched, 'index', split_axis=0, concat_axis=0, tiled=True)]
    all_gather x1 -> x0, blocking collectives: 26.5 us -> none  [local(): lax.all_gather(query_codes, 'index', axis=0, tiled=True)]
    dot_general x9 -> x0, matrix products: 17.6 us -> none  [the longest x1 5.22 us: local(): lax.dot_general(sign_bits, bank_codes, (((1,), (1,)), ((), ())), preferre...]
    gather x3 -> x0, local copies, waits for them, and re-layouts: 17 us -> none  [the longest x2 13.7 us: local(): fetched = jnp.take(bank_emb, asked_offsets.reshape(-1), axis=0)]
    scatter x1 -> x0, local copies, waits for them, and re-layouts: 12.7 us -> none  [local(): jnp.zeros((shards, capacity), jnp.int32).at[owner_of, position].set(offset)]
  transfers between devices with their start and end apart: 3 -> 0, of which waited for: 2 -> 0; matrix products, arithmetic and copies ran while one was open for 13% -> 0% of each run, Pallas kernels for 0% -> 0%
where the time goes in v2:
time: 57.8 us; the launch traced here: 57.6 us
  Pallas kernels  56.9 us (98%)
  between operations  0.64 us (1%)
    pallas_call x1, Pallas kernels, whole(): pl.pallas_call(whole_kernel, out_shape=(jax.ShapeDtypeStruct((16, 128), j...  55.4 us
    pallas_call x1, Pallas kernels, emit(): pl.pallas_call(emit_kernel, out_shape=(jax.ShapeDtypeStruct((16, 16), jnp...  1.54 us

profile of v2, /device:TPU:1, one launch (start us, length us, event | category | flops | bytes accessed | tf_op | source)
XLA Modules:
  0.0 57.6 jit_solution(6917570406905755895)
XLA Ops:
  0.6 55.4 %whole.1 = (s32[16,128]{1,0:T(8,128)}, bf16[32,1024]{1,0:T(8,128)(2,1)}, f32[8,1024]{1,0:T(8,128)}) custom-call(s32[16,64]{1,0:T(8,128)} %qcodes_ref.1, s32[1,16]{1,0:T(1,128)} %bitcast.1, s32[16,16]{1,0:T(8,128)} %neg_ref.1, bf16[2048,1024]{1,0:T(8,128)(2,1)} %codes_hbm.1, bf16[2048,1024]{1,0:T(8,128)(2,1)} %bank_hbm.1, bf16[16,1024]{1,0:T(8,128)(2,1)} %query_ref.1, ...), custom_call_target="tpu_custom_call" | custom-call | tf_op jit(solution)/shard_map/whole/pallas_call | solution.py:491
  56.0 1.5 %emit.1 = (s32[16,16]{1,0:T(8,128)}, s32[16,16]{1,0:T(8,128)}, bf16[16,1024]{1,0:T(8,128)(2,1)}, bf16[16,1024]{1,0:T(8,128)(2,1)}, f32[8,1024]{1,0:T(8,128)}) custom-call(s32[16,128]{1,0:T(8,128)} %get-tuple-element.8.best_ref, bf16[32,1024]{1,0:T(8,128)(2,1)} %get-tuple-element.9.grads_ref, f32[8,1024]{1,0:T(8,128)} %get-tuple-element.10.sums_ref), custom_call_target="tpu_custom_call" | custom-call | tf_op jit(solution)/shard_map/emit/pallas_call | solution.py:572

commit v3 on v2

--- a/solution.py
+++ b/solution.py
@@ -159,6 +159,7 @@
 
 PORTIONS = ((0, 0, 4, (0, 1, 2)), (1, 0, 4, (1, 2, 0)), (2, 0, 4, (2, 0, 1)), (3, 0, 2, (0, 1, 2)), (3, 2, 2, (1, 0, 2)))
 TAIL = (0, 1, 2, 3, 3)
+STEPS = (2, 1, 3, 0)
 
 
 def extents(p, stage):
@@ -172,12 +173,13 @@
 
 
 def whole_kernel(
-    qcodes_ref, pos_ref, neg_ref, codes_hbm, bank_hbm, query_ref, positive_ref, head_hbm,
-    best_ref, grads_ref, hg_ref,
+    qcodes_hbm, pos_hbm, neg_hbm, codes_hbm, bank_hbm, query_hbm, positive_hbm, head_hbm,
+    ids_ref, dist_ref, qg_ref, pg_ref, hg_ref,
+    qcodes, pos_in, neg_in,
     bank, codes, head, pay, owned, out_buf, in_buf, bsend, brecv, esend, eown, ecore, s1, r2a, r2b, s2a, s2b, r3a, r3b,
-    signs, keys, pos, shard_best, crecv, packed, xs, dz, unit, inv, u_hi, u_lo,
+    signs, keys, pos, shard_best, crecv, packed, square, xs, dz, unit, inv, u_hi, u_lo,
     hs, core_in, parts, in1, mid, in2, tail, in3,
-    load_sem, p_sem, b_sem, t_sem, c_sem, x_send, x_recv, h_send, h_recv, r_send, r_recv,
+    load_sem, small_sem, p_sem, b_sem, t_sem, c_sem, x_send, x_recv, h_send, h_recv, r_send, r_recv,
 ):
     z, me, x, y, c = coords()
     others = peers(x, y, c)
@@ -185,6 +187,20 @@
     load_bank = pltpu.make_async_copy(bank_hbm, bank, load_sem.at[0])
     load_codes = pltpu.make_async_copy(codes_hbm, codes, load_sem.at[1])
     load_head = pltpu.make_async_copy(head_hbm, head, load_sem.at[2])
+    small = [
+        pltpu.make_async_copy(source, target, small_sem.at[i])
+        for i, (source, target) in enumerate(
+            (
+                (neg_hbm, neg_in),
+                (pos_hbm, pos_in),
+                (qcodes_hbm, qcodes),
+                (query_hbm, xs.at[pl.ds(0, 16)]),
+                (positive_hbm, xs.at[pl.ds(16, 16)]),
+            )
+        )
+    ]
+    for load in small:
+        load.start()
     load_bank.start()
     barrier = pltpu.get_barrier_semaphore()
     for peer in others:
@@ -195,8 +211,10 @@
     load_head.start()
 
     pay[...] = jnp.zeros((16, 128), F32)
-    pay[:, 0:64] = qcodes_ref[...].astype(F32)
-    id_col, owned_by, common = request_table(pay[...], pos_ref[...].astype(F32), neg_ref[...].astype(F32))
+    for load in small[:3]:
+        load.wait()
+    pay[:, 0:64] = qcodes[...].astype(F32)
+    id_col, owned_by, common = request_table(pay[...], pos_in[...].astype(F32), neg_in[...].astype(F32))
     owned[...] = owned_by
     lane = iota((32, 8, 128), 2)
     base_cols = jnp.broadcast_to(id_col[0:256], (256, 128)).reshape(32, 8, 128)
@@ -207,8 +225,8 @@
         copy_to(out_buf.at[peer], in_buf.at[me], p_sem.at[0], p_sem.at[1], (z, peer)).start()
     in_buf[me] = out_buf[me]
 
-    xs[0:16] = query_ref[...]
-    xs[16:32] = positive_ref[...]
+    for load in small[3:]:
+        load.wait()
 
     def project(start, count):
         rows = slice(start, start + count)
@@ -253,11 +271,16 @@
     s1[...] = (eown[...].astype(F32) + ecore[...].astype(F32)).astype(BF16).reshape(4, 4, 32, 1024)
 
     left, right = pl.ds(0, 512), pl.ds(512, 512)
-    for k in (2, 1, 3):
-        to = lax.rem(x + k, SIDE)
-        copy_to(s1.at[to, :, :, left], r2a.at[k - 1], x_send.at[0], x_recv.at[0], (z, at(to, y, c))).start()
-        to = lax.rem(y + k, SIDE)
-        copy_to(s1.at[:, to, :, right], r2b.at[k - 1], x_send.at[1], x_recv.at[1], (z, at(x, to, c))).start()
+    for j in (2, 1, 3, 0):
+        xj, yj = lax.rem(x + j, SIDE), lax.rem(y + j, SIDE)
+        for k in (2, 1, 3):
+            xk, yk = lax.rem(x + k, SIDE), lax.rem(y + k, SIDE)
+            copy_to(
+                s1.at[xk, yj, :, left], r2a.at[j, k - 1], x_send.at[0, j], x_recv.at[0, j], (z, at(xk, y, c))
+            ).start()
+            copy_to(
+                s1.at[xj, yk, :, right], r2b.at[j, k - 1], x_send.at[1, j], x_recv.at[1, j], (z, at(x, yk, c))
+            ).start()
 
     signs_v, pos_v = sign_rows(in_buf[...].reshape(512, 128))
     signs[...] = signs_v
@@ -294,27 +317,28 @@
         for i in range(16):
             shard_best[t, i : i + 1, :] = best[i][0:1, :]
 
-    select(0)
-    select(1)
-
     def total(own, got):
         t = own.astype(F32)
         for k in range(SIDE - 1):
             t = t + got[k].astype(F32)
         return t
 
-    take(r2a, x_recv.at[0])
-    take(r2b, x_recv.at[1])
-    s2a[...] = total(s1[x, :, :, 0:512], r2a).astype(BF16)
-    s2b[...] = total(s1[:, y, :, 512:1024], r2b).astype(BF16)
-    for k in (2, 1, 3):
-        to = lax.rem(y + k, SIDE)
-        copy_to(s2a.at[to], r3a.at[k - 1], x_send.at[2], x_recv.at[2], (z, at(x, to, c))).start()
-        to = lax.rem(x + k, SIDE)
-        copy_to(s2b.at[to], r3b.at[k - 1], x_send.at[3], x_recv.at[3], (z, at(to, y, c))).start()
-
+    def pass_on(j):
+        xj, yj = lax.rem(x + j, SIDE), lax.rem(y + j, SIDE)
+        take(r2a.at[j], x_recv.at[0, j])
+        s2a[j] = total(s1[x, yj, :, 0:512], r2a.at[j]).astype(BF16)
+        copy_to(s2a.at[j], r3a.at[j - 1], x_send.at[0, 4], x_recv.at[0, 4], (z, at(x, yj, c))).start()
+        take(r2b.at[j], x_recv.at[1, j])
+        s2b[j] = total(s1[xj, y, :, 512:1024], r2b.at[j]).astype(BF16)
+        copy_to(s2b.at[j], r3b.at[j - 1], x_send.at[1, 4], x_recv.at[1, 4], (z, at(xj, y, c))).start()
+
+    select(0)
+    select(1)
+    pass_on(2)
     select(2)
+    pass_on(1)
     select(3)
+    pass_on(3)
     for peer in others:
         copy_to(shard_best.at[lax.div(peer, 8)], crecv.at[me], t_sem.at[0], t_sem.at[1], (z, peer)).start()
     crecv[me] = shard_best[lax.div(me, 8)]
@@ -324,10 +348,14 @@
     xs[32:288, 0:512] = got[:, 0:8].reshape(256, 512).astype(BF16)
     xs[32:288, 512:1024] = got[:, 8:16].reshape(256, 512).astype(BF16)
     project(32, 256)
-    take(r3a, x_recv.at[2])
-    take(r3b, x_recv.at[3])
-    xs[288:320, 0:512] = total(s2a[y], r3a).astype(BF16)
-    xs[288:320, 512:1024] = total(s2b[x], r3b).astype(BF16)
+    take(r2a.at[0], x_recv.at[0, 0])
+    own_left = total(s1[x, y, :, 0:512], r2a.at[0])
+    take(r2b.at[0], x_recv.at[1, 0])
+    own_right = total(s1[x, y, :, 512:1024], r2b.at[0])
+    take(r3a, x_recv.at[0, 4])
+    xs[288:320, 0:512] = total(own_left, r3a).astype(BF16)
+    take(r3b, x_recv.at[1, 4])
+    xs[288:320, 512:1024] = total(own_right, r3b).astype(BF16)
     project(288, 32)
 
     q_hi, q_lo = u_hi[0:16], u_lo[0:16]
@@ -349,25 +377,18 @@
     along = dot(k1_hi, q_hi) + (dot(k1_lo, q_hi) + dot(k1_hi, q_lo))
     dz[16:320] = (along - unit[16:320] * k2).astype(BF16)
 
-    def piece(i):
-        m = lax.rem(2 * (z + 1) + i, 8)
-        return m, lax.div(m, 2), pl.ds(lax.rem(m, 2) * 2, 2)
-
     def h_copy(i):
-        m, zz, xx = piece(i)
-        return copy_to(hs.at[1 - c, zz, xx], core_in.at[zz, xx], h_send, h_recv.at[m], partner)
-
-    def grow(i, carry):
-        m, zz, xx = piece(i)
-        part = dot(xs[:, pl.ds(pl.multiple_of(m * 128, 128), 128)], dz[...], firsts).reshape(16, 8, 1024)
+        zz = lax.rem(z + STEPS[i], SIDE)
+        return copy_to(hs.at[1 - c, zz], core_in.at[zz], h_send, h_recv.at[i], partner)
+
+    def grow(i):
+        zz = lax.rem(z + STEPS[i], SIDE)
+        part = dot(xs[:, pl.ds(pl.multiple_of(zz * 256, 256), 256)], dz[...], firsts).reshape(32, 8, 1024)
         part = jnp.concatenate([part[:, :, 0:512], part[:, :, 512:1024]], axis=1).astype(BF16)
-        part = part.reshape(2, 4, 2, 16, 512)
+        part = part.reshape(4, 4, 2, 16, 512)
         for core in range(2):
-            hs[core, zz, xx] = part[:, :, core]
+            hs[core, zz] = part[:, :, core]
         h_copy(i).start()
-        return carry
-
-    lax.fori_loop(0, 8, grow, 0)
 
     place = (z, x, y)
 
@@ -385,25 +406,39 @@
             index[order[0]] = to
         return (*index, slice(None), pl.ds(tile * 128, 128))
 
-    def send_first(p, k):
-        axis = PORTIONS[p][3][0]
-        to = lax.rem(place[axis] + k, SIDE)
-        copy_to(
-            parts.at[first_from(p, to)], in1[p].at[k - 1], r_send.at[0, p], r_recv.at[0, p], device(axis, to)
-        ).start()
-
-    for i in range(8):
-        m, zz, xx = piece(i)
+    def gather_core(i):
+        zz = lax.rem(z + STEPS[i], SIDE)
         h_copy(i).wait_recv()
-        parts[zz, xx] = (hs[c, zz, xx].astype(F32) + core_in[zz, xx].astype(F32)).astype(BF16)
-        if i % 2 == 1 and i < 6:
-            send_first(0, i // 2 + 1)
-            send_first(3, i // 2 + 1)
-    for k in (2, 1, 3):
-        for p in (1, 4, 2):
-            send_first(p, k)
-
-    grads_ref[...] = dot(dz[0:32], head[...], LAST).astype(BF16)
+        parts[zz] = (hs[c, zz].astype(F32) + core_in[zz].astype(F32)).astype(BF16)
+        for p in (3, 4, 0, 1, 2):
+            tile, y0, ys, order = PORTIONS[p]
+            lanes = pl.ds(tile * 128, 128)
+            if order[0] == 0:
+                moves = [(zz, parts.at[zz, :, pl.ds(y0, ys), :, lanes], in1[p].at[STEPS[i] - 1])] if STEPS[i] else []
+            else:
+                moves = []
+                for k in (2, 1, 3):
+                    to = lax.rem(place[order[0]] + k, SIDE)
+                    if order[0] == 1:
+                        source = parts.at[zz, to, pl.ds(y0, ys), :, lanes]
+                    else:
+                        source = parts.at[zz, :, to, :, lanes]
+                    moves.append((to, source, in1[p].at[k - 1, zz]))
+            for to, source, target in moves:
+                copy_to(source, target, r_send.at[0, p], r_recv.at[0, p], device(order[0], to)).start()
+
+    grow(0)
+    grow(1)
+    gather_core(0)
+    grow(2)
+    gather_core(1)
+    grow(3)
+    gather_core(2)
+    gather_core(3)
+
+    grads = dot(dz[0:32], head[...], LAST).astype(BF16)
+    qg_ref[...] = grads[0:16]
+    pg_ref[...] = grads[16:32]
 
     take(crecv.at[pl.ds(0, GROUP - 1)], t_sem.at[1])
     lane = iota((16, 128), 1)
@@ -422,8 +457,12 @@
         best = merge16(best, [pltpu.roll(b, d, 1) for b in best])
     for d in (6, 7):
         best = merge16(best, [pltpu.roll(b, d, 0) for b in best])
+    square[...] = jnp.zeros((128, 128), jnp.int32)
     for i in range(16):
-        best_ref[i : i + 1, :] = best[i][0:1, :]
+        square[i : i + 1, :] = best[i][0:1, :]
+    flat = square[...]
+    ids_ref[...] = jnp.transpose((flat & 65535).astype(F32))[0:16, 0:16].astype(jnp.int32)
+    dist_ref[...] = jnp.transpose((flat >> 16).astype(F32))[0:16, 0:16].astype(jnp.int32)
 
     def pick(p, stage, to):
         axis = PORTIONS[p][3][stage]
@@ -467,10 +506,11 @@
     take(bsend.at[pl.ds(0, GROUP - 1)], b_sem.at[0])
     take(crecv.at[pl.ds(0, GROUP - 1)], t_sem.at[0])
     core_copy.wait_send()
-    take(r2a, x_send.at[0])
-    take(r2b, x_send.at[1])
-    take(r3a, x_send.at[2])
-    take(r3b, x_send.at[3])
+    for j in range(SIDE):
+        take(r2a.at[j], x_send.at[0, j])
+        take(r2b.at[j], x_send.at[1, j])
+    take(r3a, x_send.at[0, 4])
+    take(r3b, x_send.at[1, 4])
     take(core_in, h_send)
     for p in range(5):
         take(in1[p], r_send.at[0, p])
@@ -491,13 +531,18 @@
     return pl.pallas_call(
         whole_kernel,
         out_shape=(
-            jax.ShapeDtypeStruct((16, 128), jnp.int32),
-            jax.ShapeDtypeStruct((32, 1024), BF16),
+            jax.ShapeDtypeStruct((16, 16), jnp.int32),
+            jax.ShapeDtypeStruct((16, 16), jnp.int32),
+            jax.ShapeDtypeStruct((16, 1024), BF16),
+            jax.ShapeDtypeStruct((16, 1024), BF16),
             jax.ShapeDtypeStruct((8, 1024), F32),
         ),
-        in_specs=[vm, vm, vm, anywhere, anywhere, vm, vm, anywhere],
-        out_specs=(vm,) * 3,
+        in_specs=[anywhere] * 8,
+        out_specs=(vm,) * 5,
         scratch_shapes=[
+            pltpu.VMEM((16, 64), jnp.int32),
+            pltpu.VMEM((1, 16), jnp.int32),
+            pltpu.VMEM((16, 16), jnp.int32),
             pltpu.VMEM((2048, 1024), BF16),
             pltpu.VMEM((2048, 1024), BF16),
             pltpu.VMEM((1024, 1024), BF16),
@@ -511,8 +556,8 @@
             pltpu.VMEM((16, 32, 1024), BF16),
             pltpu.VMEM((16, 32, 1024), BF16),
             pltpu.VMEM((4, 4, 32, 1024), BF16),
-            pltpu.VMEM((3, 4, 32, 512), BF16),
-            pltpu.VMEM((3, 4, 32, 512), BF16),
+            pltpu.VMEM((4, 3, 32, 512), BF16),
+            pltpu.VMEM((4, 3, 32, 512), BF16),
             pltpu.VMEM((4, 32, 512), BF16),
             pltpu.VMEM((4, 32, 512), BF16),
             pltpu.VMEM((3, 32, 512), BF16),
@@ -523,6 +568,7 @@
             pltpu.VMEM((4, 16, 128), F32),
             pltpu.VMEM((32, 16, 128), F32),
             pltpu.VMEM((8, 16, 128), jnp.int32),
+            pltpu.VMEM((128, 128), jnp.int32),
             pltpu.VMEM((320, 1024), BF16),
             pltpu.VMEM((320, 1024), BF16),
             pltpu.VMEM((320, 1024), F32),
@@ -538,14 +584,15 @@
             pltpu.VMEM((4, 4, *block), BF16),
             pltpu.VMEM((4, 3, *block), BF16),
             dma((3,)),
+            dma((5,)),
             dma((2,)),
             dma((2,)),
             dma((2,)),
             dma((2,)),
+            dma((2, 5)),
+            dma((2, 5)),
+            dma,
             dma((4,)),
-            dma((4,)),
-            dma,
-            dma((8,)),
             dma((3, 5)),
             dma((3, 5)),
         ],
@@ -556,33 +603,25 @@
     )(codes, pos, neg, bank_codes, bank_emb, query_emb, positive_emb, head)
 
 
-def emit_kernel(best_ref, grads_ref, sums_ref, ids_ref, dist_ref, qg_ref, pg_ref, hg_ref, square):
-    square[...] = jnp.zeros((128, 128), jnp.int32)
-    square[0:16, :] = best_ref[...]
-    flat = square[...]
-    ids_ref[...] = jnp.transpose((flat & 65535).astype(F32))[0:16, 0:16].astype(jnp.int32)
-    dist_ref[...] = jnp.transpose((flat >> 16).astype(F32))[0:16, 0:16].astype(jnp.int32)
-    qg_ref[...] = grads_ref[0:16]
-    pg_ref[...] = grads_ref[16:32]
-    hg_ref[...] = sums_ref[...]
-
-
-def emit(best, grads, sums):
-    vm = pl.BlockSpec(memory_space=pltpu.VMEM)
+def emit_kernel(*refs):
+    sources, targets, sem = refs[0:5], refs[5:10], refs[10]
+    copies = [pltpu.make_async_copy(a, b, sem.at[i]) for i, (a, b) in enumerate(zip(sources, targets))]
+    for copy in copies:
+        copy.start()
+    for copy in copies:
+        copy.wait()
+
+
+def emit(*arrays):
+    anywhere = pl.BlockSpec(memory_space=pl.ANY)
     return pl.pallas_call(
         emit_kernel,
-        out_shape=(
-            jax.ShapeDtypeStruct((16, 16), jnp.int32),
-            jax.ShapeDtypeStruct((16, 16), jnp.int32),
-            jax.ShapeDtypeStruct((16, 1024), BF16),
-            jax.ShapeDtypeStruct((16, 1024), BF16),
-            jax.ShapeDtypeStruct((8, 1024), F32),
-        ),
-        in_specs=[vm] * 3,
-        out_specs=(vm,) * 5,
-        scratch_shapes=[pltpu.VMEM((128, 128), jnp.int32)],
+        out_shape=tuple(jax.ShapeDtypeStruct(a.shape, a.dtype) for a in arrays),
+        in_specs=[anywhere] * 5,
+        out_specs=(anywhere,) * 5,
+        scratch_shapes=[pltpu.SemaphoreType.DMA((5,))],
         name="emit",
-    )(best, grads, sums)
+    )(*arrays)
 
 
 def local(

time: 57.8 us -> 58.5 us (1.012)
  no operation moved by 1% of the time
where the time goes in v3:
time: 58.5 us; the launch traced here: 57.9 us
  Pallas kernels  57.1 us (98%)
  between operations  0.8 us (1%)
    pallas_call x1, Pallas kernels, whole(): pl.pallas_call(whole_kernel, out_shape=(jax.ShapeDtypeStruct((16, 16), jn...  52.5 us
    pallas_call x1, Pallas kernels, emit(): pl.pallas_call(emit_kernel, out_shape=tuple((jax.ShapeDtypeStruct(a.shape...  4.62 us

profile of v3, /device:TPU:1, one launch (start us, length us, event | category | flops | bytes accessed | tf_op | source)
XLA Modules:
  0.0 57.9 jit_solution(41300416096756181)
XLA Ops:
  0.6 52.5 %whole.1 = (s32[16,16]{1,0:T(8,128)}, s32[16,16]{1,0:T(8,128)}, bf16[16,1024]{1,0:T(8,128)(2,1)}, bf16[16,1024]{1,0:T(8,128)(2,1)}, f32[8,1024]{1,0:T(8,128)}) custom-call(s32[16,64]{1,0:T(8,128)} %qcodes_hbm.1, s32[1,16]{1,0:T(1,128)} %bitcast.1, s32[16,16]{1,0:T(8,128)} %neg_hbm.1, bf16[2048,1024]{1,0:T(8,128)(2,1)} %codes_hbm.1, ...), custom_call_target="tpu_custom_call" | custom-call | tf_op jit(solution)/shard_map/whole/pallas_call | solution.py:531
  53.1 4.6 %emit.1 = (s32[16,16]{1,0:T(8,128)}, s32[16,16]{1,0:T(8,128)}, bf16[16,1024]{1,0:T(8,128)(2,1)}, bf16[16,1024]{1,0:T(8,128)(2,1)}, f32[8,1024]{1,0:T(8,128)}) custom-call(s32[16,16]{1,0:T(8,128)} %get-tuple-element.10.refs_0_, s32[16,16]{1,0:T(8,128)} %get-tuple-element.11.refs_1_, bf16[16,1024]{1,0:T(8,128)(2,1)} %get-tuple-element.12.refs_2_, ...), custom_call_target="tpu_custom_call" | custom-call | tf_op jit(solution)/shard_map/emit/pallas_call | solution.py:617

commit v4 on v3

--- a/solution.py
+++ b/solution.py
@@ -63,7 +63,7 @@
     pltpu.make_async_copy(ref, ref, sem).wait()
 
 
-def request_table(codes, pos_row, negatives):
+def request_table(pos_row, negatives):
     hi = jnp.floor(negatives * (1.0 / 256.0))
     lo = negatives - 256.0 * hi
     halves = jnp.concatenate([hi, lo], axis=0).astype(BF16)
@@ -89,12 +89,7 @@
     ext_row = jnp.sum(
         jnp.where(lane32 == sub32 + 96, jnp.broadcast_to(id_col[256:288], (32, 128)), 0.0), axis=0, keepdims=True
     )
-    diagonal = iota((16, 16), 0) == iota((16, 16), 1)
-    pos_col = jnp.sum(jnp.where(diagonal, jnp.broadcast_to(pos_row, (16, 16)), 0.0), axis=1, keepdims=True)
-    lane16 = iota((16, 128), 1)
-    rest = jnp.where(lane16 >= 96, jnp.broadcast_to(ext_row, (16, 128)), 0.0)
-    rest = jnp.where(lane16 == 64, jnp.broadcast_to(pos_col, (16, 128)), rest)
-    return id_col, owned_by, jnp.where(lane16 < 64, codes, rest)
+    return id_col, owned_by, ext_row
 
 
 def onehot_rows(rel, count):
@@ -151,10 +146,7 @@
     pick = jnp.where(lane == source, 1.0, 0.0).astype(BF16)
     byte = dot(pick, both, LAST).astype(jnp.int32)
     bit = byte & (1 << (iota((1024, 512), 0) & 7))
-    signs = jnp.where(bit != 0, -1024.0, 1024.0).astype(BF16)
-    lane16 = iota((16, 256), 1)
-    weigh = jnp.where(lane16 == 64, 256.0, jnp.where(lane16 == 192, 1.0, 0.0)).astype(BF16)
-    return signs, dot(weigh, both, LAST)
+    return jnp.where(bit != 0, -1024.0, 1024.0).astype(BF16)
 
 
 PORTIONS = ((0, 0, 4, (0, 1, 2)), (1, 0, 4, (1, 2, 0)), (2, 0, 4, (2, 0, 1)), (3, 0, 2, (0, 1, 2)), (3, 2, 2, (1, 0, 2)))
@@ -174,12 +166,12 @@
 
 def whole_kernel(
     qcodes_hbm, pos_hbm, neg_hbm, codes_hbm, bank_hbm, query_hbm, positive_hbm, head_hbm,
-    ids_ref, dist_ref, qg_ref, pg_ref, hg_ref,
-    qcodes, pos_in, neg_in,
-    bank, codes, head, pay, owned, out_buf, in_buf, bsend, brecv, esend, eown, ecore, s1, r2a, r2b, s2a, s2b, r3a, r3b,
-    signs, keys, pos, shard_best, crecv, packed, square, xs, dz, unit, inv, u_hi, u_lo,
+    out_hbm,
+    qcodes, pos_in, neg_in, out_v,
+    bank, codes, head, pay, owned, out_buf, in_buf, code_out, code_in, bsend, brecv, esend, eown, ecore, s1, r2a, r2b, s2a, s2b, r3a, r3b,
+    signs, keys, pos, shard_best, crecv, packed, square, xs, dz, raw, unit, inv, u_hi, u_lo,
     hs, core_in, parts, in1, mid, in2, tail, in3,
-    load_sem, small_sem, p_sem, b_sem, t_sem, c_sem, x_send, x_recv, h_send, h_recv, r_send, r_recv,
+    load_sem, small_sem, p_sem, q_sem, b_sem, t_sem, c_sem, x_send, x_recv, h_send, h_recv, r_send, r_recv,
 ):
     z, me, x, y, c = coords()
     others = peers(x, y, c)
@@ -210,20 +202,25 @@
     load_codes.start()
     load_head.start()
 
-    pay[...] = jnp.zeros((16, 128), F32)
     for load in small[:3]:
         load.wait()
-    pay[:, 0:64] = qcodes[...].astype(F32)
-    id_col, owned_by, common = request_table(pay[...], pos_in[...].astype(F32), neg_in[...].astype(F32))
+    pay[...] = jnp.zeros((8, 128), F32)
+    pay[:, 64:80] = jnp.broadcast_to(pos_in[...].astype(F32), (8, 16))
+    code_out[...] = jnp.zeros((16, 128), F32)
+    code_out[:, 0:64] = qcodes[...].astype(F32)
+    id_col, owned_by, ext_row = request_table(pos_in[...].astype(F32), neg_in[...].astype(F32))
     owned[...] = owned_by
-    lane = iota((32, 8, 128), 2)
+    lane8 = iota((8, 128), 1)
+    common = jnp.where(lane8 >= 96, jnp.broadcast_to(ext_row, (8, 128)), pay[...])
     base_cols = jnp.broadcast_to(id_col[0:256], (256, 128)).reshape(32, 8, 128)
-    out_buf[:, 0:8, :] = jnp.where(lane == 65, base_cols, jnp.broadcast_to(common[None, 0:8], (32, 8, 128)))
-    out_buf[:, 8:16, :] = jnp.broadcast_to(common[None, 8:16], (32, 8, 128))
+    out_buf[...] = jnp.where(iota((32, 8, 128), 2) == 0, base_cols, jnp.broadcast_to(common[None], (32, 8, 128)))
     pl.semaphore_wait(barrier, len(others) + SIDE - 1)
     for peer in others:
         copy_to(out_buf.at[peer], in_buf.at[me], p_sem.at[0], p_sem.at[1], (z, peer)).start()
+    for peer in others:
+        copy_to(code_out, code_in.at[me], q_sem.at[0], q_sem.at[1], (z, peer)).start()
     in_buf[me] = out_buf[me]
+    code_in[me] = code_out[...]
 
     for load in small[3:]:
         load.wait()
@@ -245,8 +242,8 @@
     take(in_buf.at[pl.ds(0, GROUP - 1)], p_sem.at[1])
 
     first = (me * 2048).astype(F32)
-    asked = in_buf[:, 0:8, :].reshape(256, 128)
-    base_rel = jnp.sum(jnp.where(iota((256, 128), 1) == 65, asked, 0.0), axis=1, keepdims=True) - first
+    asked = in_buf[...].reshape(256, 128)
+    base_rel = jnp.sum(jnp.where(iota((256, 128), 1) == 0, asked, 0.0), axis=1, keepdims=True) - first
     hot = onehot_rows(base_rel, 256)
     for h in range(2):
         part = dot(hot, bank[:, h * 512 : (h + 1) * 512])
@@ -282,9 +279,15 @@
                 s1.at[xj, yk, :, right], r2b.at[j, k - 1], x_send.at[1, j], x_recv.at[1, j], (z, at(x, yk, c))
             ).start()
 
-    signs_v, pos_v = sign_rows(in_buf[...].reshape(512, 128))
-    signs[...] = signs_v
-    pos[...] = pos_v[0:8] - first
+    take(code_in.at[pl.ds(0, GROUP - 1)], q_sem.at[1])
+    signs[...] = sign_rows(code_in[...].reshape(512, 128))
+    lane8 = iota((8, 128), 1)
+    for t in range(4):
+        row = jnp.zeros((8, 128), F32)
+        for i in range(8):
+            ids = pltpu.roll(in_buf[8 * t + i], (16 * i + 64) % 128, 1)
+            row = jnp.where((lane8 >> 4) == i, ids, row)
+        pos[:, t * 128 : (t + 1) * 128] = row - first
     load_codes.wait()
 
     def product(m, carry):
@@ -332,8 +335,40 @@
         s2b[j] = total(s1[xj, y, :, 512:1024], r2b.at[j]).astype(BF16)
         copy_to(s2b.at[j], r3b.at[j - 1], x_send.at[1, 4], x_recv.at[1, 4], (z, at(xj, y, c))).start()
 
+    firsts = (((0,), (0,)), ((), ()))
+    own_pos = jnp.where(iota((16, 16), 0) == iota((16, 16), 1), 1.0, 0.0)
+    q_unit, q_hi, q_lo = unit[0:16], u_hi[0:16], u_lo[0:16]
+
+    def column(row):
+        return jnp.sum(own_pos * jnp.broadcast_to(row, (16, 16)), axis=1, keepdims=True)
+
+    def scores(start, count, mask):
+        rows = slice(start, start + count)
+        high, low = u_hi[rows], u_lo[rows]
+        logits = 50.0 * (dot(high, q_hi, LAST) + (dot(low, q_hi, LAST) + dot(high, q_lo, LAST)))
+        logits = jnp.where(mask > 0.5, logits, 0.0)
+        return logits, jnp.where(mask > 0.5, jnp.exp(logits), 0.0)
+
+    def negatives(start, count):
+        rows = slice(start, start + count)
+        logits, w = scores(start, count, owned[start - 32 : start - 32 + count, 0:16])
+        w_hi, w_lo = split(w)
+        high, low = u_hi[rows], u_lo[rows]
+        along = dot(w_hi, high, firsts) + (dot(w_lo, high, firsts) + dot(w_hi, low, firsts))
+        scale = inv[rows, 0:1]
+        k_hi, k_lo = split(w * (50.0 * scale))
+        pull = dot(k_hi, q_hi) + (dot(k_lo, q_hi) + dot(k_hi, q_lo))
+        k2 = jnp.sum(w * logits, axis=1, keepdims=True) * scale
+        raw[start - 32 : start - 32 + count] = pull - unit[rows] * k2
+        return jnp.sum(w, axis=0, keepdims=True), along
+
     select(0)
     select(1)
+    take(brecv.at[pl.ds(0, GROUP - 1)], b_sem.at[1])
+    got = brecv[...].astype(F32)
+    xs[32:288, 0:512] = got[:, 0:8].reshape(256, 512).astype(BF16)
+    xs[32:288, 512:1024] = got[:, 8:16].reshape(256, 512).astype(BF16)
+    project(32, 256)
     pass_on(2)
     select(2)
     pass_on(1)
@@ -342,12 +377,9 @@
     for peer in others:
         copy_to(shard_best.at[lax.div(peer, 8)], crecv.at[me], t_sem.at[0], t_sem.at[1], (z, peer)).start()
     crecv[me] = shard_best[lax.div(me, 8)]
-
-    take(brecv.at[pl.ds(0, GROUP - 1)], b_sem.at[1])
-    got = brecv[...].astype(F32)
-    xs[32:288, 0:512] = got[:, 0:8].reshape(256, 512).astype(BF16)
-    xs[32:288, 512:1024] = got[:, 8:16].reshape(256, 512).astype(BF16)
-    project(32, 256)
+    pos_logits, pos_w = scores(16, 16, own_pos)
+    base_sum, base_along = negatives(32, 256)
+
     take(r2a.at[0], x_recv.at[0, 0])
     own_left = total(s1[x, y, :, 0:512], r2a.at[0])
     take(r2b.at[0], x_recv.at[1, 0])
@@ -357,25 +389,17 @@
     take(r3b, x_recv.at[1, 4])
     xs[288:320, 512:1024] = total(own_right, r3b).astype(BF16)
     project(288, 32)
-
-    q_hi, q_lo = u_hi[0:16], u_lo[0:16]
-    c_hi, c_lo = u_hi[16:320], u_lo[16:320]
-    logits = 50.0 * (dot(c_hi, q_hi, LAST) + (dot(c_lo, q_hi, LAST) + dot(c_hi, q_lo, LAST)))
-    own_pos = jnp.where(iota((16, 16), 0) == iota((16, 16), 1), 1.0, 0.0)
-    mask = jnp.concatenate([own_pos, owned[:, 0:16]], axis=0)
-    weights = jnp.where(mask > 0.5, jnp.exp(jnp.where(mask > 0.5, logits, 0.0)), 0.0)
-    probs = weights / jnp.sum(weights, axis=0, keepdims=True)
-    slopes = probs - jnp.concatenate([own_pos, jnp.zeros((288, 16), F32)], axis=0)
-    s_hi, s_lo = split(slopes)
-    firsts = (((0,), (0,)), ((), ()))
-    du = 50.0 * (dot(s_hi, c_hi, firsts) + (dot(s_lo, c_hi, firsts) + dot(s_hi, c_lo, firsts)))
-    q_unit = unit[0:16]
+    ext_sum, ext_along = negatives(288, 32)
+
+    share = 1.0 / (base_sum + ext_sum + jnp.sum(pos_w, axis=0, keepdims=True))
+    slot_share = jnp.sum(owned[:, 0:16] * share, axis=1, keepdims=True)
+    dz[32:320] = (raw[...] * slot_share).astype(BF16)
+    pos_slope = column(jnp.sum(pos_w, axis=0, keepdims=True) * share - 1.0)
+    pos_unit = unit[16:32]
+    du = 50.0 * (column(share) * (base_along + ext_along) + pos_slope * pos_unit)
     dz[0:16] = ((du - q_unit * jnp.sum(q_unit * du, axis=1, keepdims=True)) * inv[0:16, 0:1]).astype(BF16)
-    inv_c = inv[16:320, 0:1]
-    k1_hi, k1_lo = split(slopes * (50.0 * inv_c))
-    k2 = jnp.sum(slopes * logits, axis=1, keepdims=True) * inv_c
-    along = dot(k1_hi, q_hi) + (dot(k1_lo, q_hi) + dot(k1_hi, q_lo))
-    dz[16:320] = (along - unit[16:320] * k2).astype(BF16)
+    pos_logit = jnp.sum(pos_logits, axis=1, keepdims=True)
+    dz[16:32] = (pos_slope * (50.0 * q_unit - pos_unit * pos_logit) * inv[16:32, 0:1]).astype(BF16)
 
     def h_copy(i):
         zz = lax.rem(z + STEPS[i], SIDE)
@@ -436,9 +460,7 @@
     gather_core(2)
     gather_core(3)
 
-    grads = dot(dz[0:32], head[...], LAST).astype(BF16)
-    qg_ref[...] = grads[0:16]
-    pg_ref[...] = grads[16:32]
+    out_v[8:40] = dot(dz[0:32], head[...], LAST)
 
     take(crecv.at[pl.ds(0, GROUP - 1)], t_sem.at[1])
     lane = iota((16, 128), 1)
@@ -461,8 +483,10 @@
     for i in range(16):
         square[i : i + 1, :] = best[i][0:1, :]
     flat = square[...]
-    ids_ref[...] = jnp.transpose((flat & 65535).astype(F32))[0:16, 0:16].astype(jnp.int32)
-    dist_ref[...] = jnp.transpose((flat >> 16).astype(F32))[0:16, 0:16].astype(jnp.int32)
+    out_v[40:56, 0:128] = jnp.transpose((flat & 65535).astype(F32))[0:16]
+    out_v[40:56, 128:256] = jnp.transpose((flat >> 16).astype(F32))[0:16]
+    early = pltpu.make_async_copy(out_v.at[pl.ds(8, 48)], out_hbm.at[pl.ds(8, 48)], small_sem.at[0])
+    early.start()
 
     def pick(p, stage, to):
         axis = PORTIONS[p][3][stage]
@@ -499,10 +523,13 @@
     for q in range(4):
         take(in3.at[q], r_recv.at[2, q])
         out = total(tail[q, place[PORTIONS[q][3][2]]], in3.at[q])
-        hg_ref[:, q * 128 : (q + 1) * 128] = out[0:8]
-        hg_ref[:, 512 + q * 128 : 512 + (q + 1) * 128] = out[8:16]
+        out_v[0:8, q * 128 : (q + 1) * 128] = out[0:8]
+        out_v[0:8, 512 + q * 128 : 512 + (q + 1) * 128] = out[8:16]
+    late = pltpu.make_async_copy(out_v.at[pl.ds(0, 8)], out_hbm.at[pl.ds(0, 8)], small_sem.at[1])
+    late.start()
 
     take(out_buf.at[pl.ds(0, GROUP - 1)], p_sem.at[0])
+    take(code_in.at[pl.ds(0, GROUP - 1)], q_sem.at[0])
     take(bsend.at[pl.ds(0, GROUP - 1)], b_sem.at[0])
     take(crecv.at[pl.ds(0, GROUP - 1)], t_sem.at[0])
     core_copy.wait_send()
@@ -517,10 +544,11 @@
         take(in2[p], r_send.at[1, p])
     for q in range(4):
         take(in3.at[q], r_send.at[2, q])
+    early.wait()
+    late.wait()
 
 
 def whole(codes, pos, neg, bank_codes, bank_emb, query_emb, positive_emb, head):
-    vm = pl.BlockSpec(memory_space=pltpu.VMEM)
     anywhere = pl.BlockSpec(memory_space=pl.ANY)
     dma = pltpu.SemaphoreType.DMA
     block = (16, 128)
@@ -530,25 +558,22 @@
 
     return pl.pallas_call(
         whole_kernel,
-        out_shape=(
-            jax.ShapeDtypeStruct((16, 16), jnp.int32),
-            jax.ShapeDtypeStruct((16, 16), jnp.int32),
-            jax.ShapeDtypeStruct((16, 1024), BF16),
-            jax.ShapeDtypeStruct((16, 1024), BF16),
-            jax.ShapeDtypeStruct((8, 1024), F32),
-        ),
+        out_shape=jax.ShapeDtypeStruct((56, 1024), F32),
         in_specs=[anywhere] * 8,
-        out_specs=(vm,) * 5,
+        out_specs=anywhere,
         scratch_shapes=[
             pltpu.VMEM((16, 64), jnp.int32),
             pltpu.VMEM((1, 16), jnp.int32),
             pltpu.VMEM((16, 16), jnp.int32),
+            pltpu.VMEM((56, 1024), F32),
             pltpu.VMEM((2048, 1024), BF16),
             pltpu.VMEM((2048, 1024), BF16),
             pltpu.VMEM((1024, 1024), BF16),
+            pltpu.VMEM((8, 128), F32),
+            pltpu.VMEM((288, 128), F32),
+            pltpu.VMEM((32, 8, 128), F32),
+            pltpu.VMEM((32, 8, 128), F32),
             pltpu.VMEM((16, 128), F32),
-            pltpu.VMEM((288, 128), F32),
-            pltpu.VMEM((32, 16, 128), F32),
             pltpu.VMEM((32, 16, 128), F32),
             pltpu.VMEM((32, 16, 512), BF16),
             pltpu.VMEM((32, 16, 512), BF16),
@@ -571,6 +596,7 @@
             pltpu.VMEM((128, 128), jnp.int32),
             pltpu.VMEM((320, 1024), BF16),
             pltpu.VMEM((320, 1024), BF16),
+            pltpu.VMEM((288, 1024), F32),
             pltpu.VMEM((320, 1024), F32),
             pltpu.VMEM((320, 128), F32),
             pltpu.VMEM((320, 1024), BF16),
@@ -589,6 +615,7 @@
             dma((2,)),
             dma((2,)),
             dma((2,)),
+            dma((2,)),
             dma((2, 5)),
             dma((2, 5)),
             dma,
@@ -603,8 +630,16 @@
     )(codes, pos, neg, bank_codes, bank_emb, query_emb, positive_emb, head)
 
 
-def emit_kernel(*refs):
-    sources, targets, sem = refs[0:5], refs[5:10], refs[10]
+OUT = (((16, 16), jnp.int32), ((16, 16), jnp.int32), ((16, 1024), BF16), ((16, 1024), BF16), ((8, 1024), F32))
+
+
+def emit_kernel(packed_ref, *refs):
+    targets, held, sem = refs[0:5], refs[5:9], refs[9]
+    held[0][...] = packed_ref[40:56, 0:16].astype(jnp.int32)
+    held[1][...] = packed_ref[40:56, 128:144].astype(jnp.int32)
+    held[2][...] = packed_ref[8:24].astype(BF16)
+    held[3][...] = packed_ref[24:40].astype(BF16)
+    sources = (*held, packed_ref.at[pl.ds(0, 8)])
     copies = [pltpu.make_async_copy(a, b, sem.at[i]) for i, (a, b) in enumerate(zip(sources, targets))]
     for copy in copies:
         copy.start()
@@ -612,25 +647,22 @@
         copy.wait()
 
 
-def emit(*arrays):
-    anywhere = pl.BlockSpec(memory_space=pl.ANY)
+def emit(packed):
     return pl.pallas_call(
         emit_kernel,
-        out_shape=tuple(jax.ShapeDtypeStruct(a.shape, a.dtype) for a in arrays),
-        in_specs=[anywhere] * 5,
-        out_specs=(anywhere,) * 5,
-        scratch_shapes=[pltpu.SemaphoreType.DMA((5,))],
+        out_shape=tuple(jax.ShapeDtypeStruct(*o) for o in OUT),
+        in_specs=[pl.BlockSpec(memory_space=pltpu.VMEM)],
+        out_specs=(pl.BlockSpec(memory_space=pl.ANY),) * 5,
+        scratch_shapes=[*(pltpu.VMEM(*o) for o in OUT[:4]), pltpu.SemaphoreType.DMA((5,))],
         name="emit",
-    )(*arrays)
+    )(packed)
 
 
 def local(
     query_codes, positive_ids, negative_ids, bank_codes, bank_emb, query_emb, positive_emb, head
 ):
     return emit(
-        *whole(
-            query_codes, positive_ids.reshape(1, -1), negative_ids, bank_codes, bank_emb, query_emb, positive_emb, head
-        )
+        whole(query_codes, positive_ids.reshape(1, -1), negative_ids, bank_codes, bank_emb, query_emb, positive_emb, head)
     )
 
 

time: 58.5 us -> 54.4 us (0.930)
  Pallas kernels: 57.1 us -> 53.4 us
    pallas_call x2, Pallas kernels: 57.1 us -> 53.4 us  [the longest x1 51.8 us: whole(): pl.pallas_call(whole_kernel, out_shape=jax.ShapeDtypeStruct((56, 1024), F...]
where the time goes in v4:
time: 54.4 us; the launch traced here: 54.2 us
  Pallas kernels  53.4 us (98%)
  between operations  0.8 us (1%)
    pallas_call x1, Pallas kernels, whole(): pl.pallas_call(whole_kernel, out_shape=jax.ShapeDtypeStruct((56, 1024), F...  51.8 us
    pallas_call x1, Pallas kernels, emit(): pl.pallas_call(emit_kernel, out_shape=tuple((jax.ShapeDtypeStruct(*o) for...  1.63 us

profile of v4, /device:TPU:1, one launch (start us, length us, event | category | flops | bytes accessed | tf_op | source)
XLA Modules:
  0.0 54.2 jit_solution(794523462044838656)
XLA Ops:
  0.6 51.8 %whole.1.packed_ref = f32[56,1024]{1,0:T(8,128)} custom-call(s32[16,64]{1,0:T(8,128)} %qcodes_hbm.1, s32[1,16]{1,0:T(1,128)} %bitcast.1, s32[16,16]{1,0:T(8,128)} %neg_hbm.1, bf16[2048,1024]{1,0:T(8,128)(2,1)} %codes_hbm.1, bf16[2048,1024]{1,0:T(8,128)(2,1)} %bank_hbm.1, bf16[16,1024]{1,0:T(8,128)(2,1)} %query_hbm.1, bf16[16,1024]{1,0:T(8,128)(2,1)} %positive_hbm.1, ...), custom_call_target="tpu_custom_call" | custom-call | tf_op jit(solution)/shard_map/whole/pallas_call | solution.py:559
  52.4 1.6 %emit.1 = (s32[16,16]{1,0:T(8,128)}, s32[16,16]{1,0:T(8,128)}, bf16[16,1024]{1,0:T(8,128)(2,1)}, bf16[16,1024]{1,0:T(8,128)(2,1)}, f32[8,1024]{1,0:T(8,128)}) custom-call(f32[56,1024]{1,0:T(8,128)} %whole.1.packed_ref), custom_call_target="tpu_custom_call" | custom-call | tf_op jit(solution)/shard_map/emit/pallas_call | solution.py:651

commit v5 on v4

--- a/solution.py
+++ b/solution.py
@@ -168,10 +168,10 @@
     qcodes_hbm, pos_hbm, neg_hbm, codes_hbm, bank_hbm, query_hbm, positive_hbm, head_hbm,
     out_hbm,
     qcodes, pos_in, neg_in, out_v,
-    bank, codes, head, pay, owned, out_buf, in_buf, code_out, code_in, bsend, brecv, esend, eown, ecore, s1, r2a, r2b, s2a, s2b, r3a, r3b,
+    bank, codes, head, pay, owned, out_buf, in_buf, bsend, brecv, esend, eown, ecore, s1, r2a, r2b, s2a, s2b, r3a, r3b,
     signs, keys, pos, shard_best, crecv, packed, square, xs, dz, raw, unit, inv, u_hi, u_lo,
     hs, core_in, parts, in1, mid, in2, tail, in3,
-    load_sem, small_sem, p_sem, q_sem, b_sem, t_sem, c_sem, x_send, x_recv, h_send, h_recv, r_send, r_recv,
+    load_sem, small_sem, p_sem, b_sem, t_sem, c_sem, x_send, x_recv, h_send, h_recv, r_send, r_recv,
 ):
     z, me, x, y, c = coords()
     others = peers(x, y, c)
@@ -206,21 +206,21 @@
         load.wait()
     pay[...] = jnp.zeros((8, 128), F32)
     pay[:, 64:80] = jnp.broadcast_to(pos_in[...].astype(F32), (8, 16))
-    code_out[...] = jnp.zeros((16, 128), F32)
-    code_out[:, 0:64] = qcodes[...].astype(F32)
+    out_buf[:, 8:16, :] = jnp.broadcast_to(
+        jnp.concatenate([qcodes[0:8], qcodes[8:16]], axis=1).astype(F32)[None], (32, 8, 128)
+    )
     id_col, owned_by, ext_row = request_table(pos_in[...].astype(F32), neg_in[...].astype(F32))
     owned[...] = owned_by
     lane8 = iota((8, 128), 1)
     common = jnp.where(lane8 >= 96, jnp.broadcast_to(ext_row, (8, 128)), pay[...])
     base_cols = jnp.broadcast_to(id_col[0:256], (256, 128)).reshape(32, 8, 128)
-    out_buf[...] = jnp.where(iota((32, 8, 128), 2) == 0, base_cols, jnp.broadcast_to(common[None], (32, 8, 128)))
+    out_buf[:, 0:8, :] = jnp.where(
+        iota((32, 8, 128), 2) == 0, base_cols, jnp.broadcast_to(common[None], (32, 8, 128))
+    )
     pl.semaphore_wait(barrier, len(others) + SIDE - 1)
     for peer in others:
         copy_to(out_buf.at[peer], in_buf.at[me], p_sem.at[0], p_sem.at[1], (z, peer)).start()
-    for peer in others:
-        copy_to(code_out, code_in.at[me], q_sem.at[0], q_sem.at[1], (z, peer)).start()
     in_buf[me] = out_buf[me]
-    code_in[me] = code_out[...]
 
     for load in small[3:]:
         load.wait()
@@ -242,7 +242,7 @@
     take(in_buf.at[pl.ds(0, GROUP - 1)], p_sem.at[1])
 
     first = (me * 2048).astype(F32)
-    asked = in_buf[...].reshape(256, 128)
+    asked = in_buf[:, 0:8, :].reshape(256, 128)
     base_rel = jnp.sum(jnp.where(iota((256, 128), 1) == 0, asked, 0.0), axis=1, keepdims=True) - first
     hot = onehot_rows(base_rel, 256)
     for h in range(2):
@@ -279,13 +279,15 @@
                 s1.at[xj, yk, :, right], r2b.at[j, k - 1], x_send.at[1, j], x_recv.at[1, j], (z, at(x, yk, c))
             ).start()
 
-    take(code_in.at[pl.ds(0, GROUP - 1)], q_sem.at[1])
-    signs[...] = sign_rows(code_in[...].reshape(512, 128))
+    pairs = in_buf[:, 8:16, :]
+    signs[...] = sign_rows(
+        jnp.concatenate([pairs, pltpu.roll(pairs.reshape(256, 128), 64, 1).reshape(32, 8, 128)], axis=1).reshape(512, 128)
+    )
     lane8 = iota((8, 128), 1)
     for t in range(4):
         row = jnp.zeros((8, 128), F32)
         for i in range(8):
-            ids = pltpu.roll(in_buf[8 * t + i], (16 * i + 64) % 128, 1)
+            ids = pltpu.roll(in_buf[8 * t + i, 0:8], (16 * i + 64) % 128, 1)
             row = jnp.where((lane8 >> 4) == i, ids, row)
         pos[:, t * 128 : (t + 1) * 128] = row - first
     load_codes.wait()
@@ -362,23 +364,16 @@
         raw[start - 32 : start - 32 + count] = pull - unit[rows] * k2
         return jnp.sum(w, axis=0, keepdims=True), along
 
-    select(0)
-    select(1)
     take(brecv.at[pl.ds(0, GROUP - 1)], b_sem.at[1])
     got = brecv[...].astype(F32)
     xs[32:288, 0:512] = got[:, 0:8].reshape(256, 512).astype(BF16)
     xs[32:288, 512:1024] = got[:, 8:16].reshape(256, 512).astype(BF16)
     project(32, 256)
     pass_on(2)
-    select(2)
-    pass_on(1)
-    select(3)
-    pass_on(3)
-    for peer in others:
-        copy_to(shard_best.at[lax.div(peer, 8)], crecv.at[me], t_sem.at[0], t_sem.at[1], (z, peer)).start()
-    crecv[me] = shard_best[lax.div(me, 8)]
     pos_logits, pos_w = scores(16, 16, own_pos)
     base_sum, base_along = negatives(32, 256)
+    pass_on(1)
+    pass_on(3)
 
     take(r2a.at[0], x_recv.at[0, 0])
     own_left = total(s1[x, y, :, 0:512], r2a.at[0])
@@ -458,35 +453,16 @@
     gather_core(1)
     grow(3)
     gather_core(2)
+    select(0)
     gather_core(3)
+    select(1)
+    select(2)
+    select(3)
+    for peer in others:
+        copy_to(shard_best.at[lax.div(peer, 8)], crecv.at[me], t_sem.at[0], t_sem.at[1], (z, peer)).start()
+    crecv[me] = shard_best[lax.div(me, 8)]
 
     out_v[8:40] = dot(dz[0:32], head[...], LAST)
-
-    take(crecv.at[pl.ds(0, GROUP - 1)], t_sem.at[1])
-    lane = iota((16, 128), 1)
-    packed[...] = jnp.full((8, 16, 128), 2147483647, jnp.int32)
-    mine = lax.rem(me, 8)
-    for g in range(4):
-        merged = jnp.zeros((16, 128), jnp.int32)
-        for s in range(8):
-            key = crecv[g * 8 + s].astype(jnp.int32)
-            key = ((key >> 11) << 16) + (key & 2047) + (g * 8 + s) * 2048
-            key = pltpu.roll(key, lax.rem((s - mine + 8) * 16, 128), 1)
-            merged = jnp.where((lane >> 4) == s, key, merged)
-        packed[g] = merged
-    best = [packed[:, i, :] for i in range(16)]
-    for d in (64, 32, 16):
-        best = merge16(best, [pltpu.roll(b, d, 1) for b in best])
-    for d in (6, 7):
-        best = merge16(best, [pltpu.roll(b, d, 0) for b in best])
-    square[...] = jnp.zeros((128, 128), jnp.int32)
-    for i in range(16):
-        square[i : i + 1, :] = best[i][0:1, :]
-    flat = square[...]
-    out_v[40:56, 0:128] = jnp.transpose((flat & 65535).astype(F32))[0:16]
-    out_v[40:56, 128:256] = jnp.transpose((flat >> 16).astype(F32))[0:16]
-    early = pltpu.make_async_copy(out_v.at[pl.ds(8, 48)], out_hbm.at[pl.ds(8, 48)], small_sem.at[0])
-    early.start()
 
     def pick(p, stage, to):
         axis = PORTIONS[p][3][stage]
@@ -520,6 +496,32 @@
             copy_to(
                 tail.at[q, to], in3.at[q, k - 1], r_send.at[2, q], r_recv.at[2, q], device(axis, to)
             ).start()
+    take(crecv.at[pl.ds(0, GROUP - 1)], t_sem.at[1])
+    lane = iota((16, 128), 1)
+    packed[...] = jnp.full((8, 16, 128), 2147483647, jnp.int32)
+    mine = lax.rem(me, 8)
+    for g in range(4):
+        merged = jnp.zeros((16, 128), jnp.int32)
+        for s in range(8):
+            key = crecv[g * 8 + s].astype(jnp.int32)
+            key = ((key >> 11) << 16) + (key & 2047) + (g * 8 + s) * 2048
+            key = pltpu.roll(key, lax.rem((s - mine + 8) * 16, 128), 1)
+            merged = jnp.where((lane >> 4) == s, key, merged)
+        packed[g] = merged
+    best = [packed[:, i, :] for i in range(16)]
+    for d in (64, 32, 16):
+        best = merge16(best, [pltpu.roll(b, d, 1) for b in best])
+    for d in (6, 7):
+        best = merge16(best, [pltpu.roll(b, d, 0) for b in best])
+    square[...] = jnp.zeros((128, 128), jnp.int32)
+    for i in range(16):
+        square[i : i + 1, :] = best[i][0:1, :]
+    flat = square[...]
+    out_v[40:56, 0:128] = jnp.transpose((flat & 65535).astype(F32))[0:16]
+    out_v[40:56, 128:256] = jnp.transpose((flat >> 16).astype(F32))[0:16]
+    early = pltpu.make_async_copy(out_v.at[pl.ds(8, 48)], out_hbm.at[pl.ds(8, 48)], small_sem.at[0])
+    early.start()
+
     for q in range(4):
         take(in3.at[q], r_recv.at[2, q])
         out = total(tail[q, place[PORTIONS[q][3][2]]], in3.at[q])
@@ -529,7 +531,6 @@
     late.start()
 
     take(out_buf.at[pl.ds(0, GROUP - 1)], p_sem.at[0])
-    take(code_in.at[pl.ds(0, GROUP - 1)], q_sem.at[0])
     take(bsend.at[pl.ds(0, GROUP - 1)], b_sem.at[0])
     take(crecv.at[pl.ds(0, GROUP - 1)], t_sem.at[0])
     core_copy.wait_send()
@@ -571,9 +572,7 @@
             pltpu.VMEM((1024, 1024), BF16),
             pltpu.VMEM((8, 128), F32),
             pltpu.VMEM((288, 128), F32),
-            pltpu.VMEM((32, 8, 128), F32),
-            pltpu.VMEM((32, 8, 128), F32),
-            pltpu.VMEM((16, 128), F32),
+            pltpu.VMEM((32, 16, 128), F32),
             pltpu.VMEM((32, 16, 128), F32),
             pltpu.VMEM((32, 16, 512), BF16),
             pltpu.VMEM((32, 16, 512), BF16),
@@ -615,7 +614,6 @@
             dma((2,)),
             dma((2,)),
             dma((2,)),
-            dma((2,)),
             dma((2, 5)),
             dma((2, 5)),
             dma,

time: 54.4 us -> 53.7 us (0.987)
  Pallas kernels: 53.4 us -> 52.8 us
    pallas_call x1, Pallas kernels: 51.8 us -> 51.1 us  [whole(): pl.pallas_call(whole_kernel, out_shape=jax.ShapeDtypeStruct((56, 1024), F...]
where the time goes in v5:
time: 53.7 us; the launch traced here: 53.6 us
  Pallas kernels  52.8 us (98%)
  between operations  0.8 us (1%)
    pallas_call x1, Pallas kernels, whole(): pl.pallas_call(whole_kernel, out_shape=jax.ShapeDtypeStruct((56, 1024), F...  51.1 us
    pallas_call x1, Pallas kernels, emit(): pl.pallas_call(emit_kernel, out_shape=tuple((jax.ShapeDtypeStruct(*o) for...  1.63 us

profile of v5, /device:TPU:1, one launch (start us, length us, event | category | flops | bytes accessed | tf_op | source)
XLA Modules:
  0.0 53.6 jit_solution(2965087813164744292)
XLA Ops:
  0.6 51.1 %whole.1.packed_ref = f32[56,1024]{1,0:T(8,128)} custom-call(s32[16,64]{1,0:T(8,128)} %qcodes_hbm.1, s32[1,16]{1,0:T(1,128)} %bitcast.1, s32[16,16]{1,0:T(8,128)} %neg_hbm.1, bf16[2048,1024]{1,0:T(8,128)(2,1)} %codes_hbm.1, bf16[2048,1024]{1,0:T(8,128)(2,1)} %bank_hbm.1, bf16[16,1024]{1,0:T(8,128)(2,1)} %query_hbm.1, bf16[16,1024]{1,0:T(8,128)(2,1)} %positive_hbm.1, ...), custom_call_target="tpu_custom_call" | custom-call | tf_op jit(solution)/shard_map/whole/pallas_call | solution.py:560
  51.8 1.6 %emit.1 = (s32[16,16]{1,0:T(8,128)}, s32[16,16]{1,0:T(8,128)}, bf16[16,1024]{1,0:T(8,128)(2,1)}, bf16[16,1024]{1,0:T(8,128)(2,1)}, f32[8,1024]{1,0:T(8,128)}) custom-call(f32[56,1024]{1,0:T(8,128)} %whole.1.packed_ref), custom_call_target="tpu_custom_call" | custom-call | tf_op jit(solution)/shard_map/emit/pallas_call | solution.py:649

commit v6 on v5

--- a/solution.py
+++ b/solution.py
@@ -169,7 +169,7 @@
     out_hbm,
     qcodes, pos_in, neg_in, out_v,
     bank, codes, head, pay, owned, out_buf, in_buf, bsend, brecv, esend, eown, ecore, s1, r2a, r2b, s2a, s2b, r3a, r3b,
-    signs, keys, pos, shard_best, crecv, packed, square, xs, dz, raw, unit, inv, u_hi, u_lo,
+    signs, keys, pos, shard_best, crecv, packed, square, xs, dz, raw, unit, inv, u_hi, u_lo, u_qq, u_qqq,
     hs, core_in, parts, in1, mid, in2, tail, in3,
     load_sem, small_sem, p_sem, b_sem, t_sem, c_sem, x_send, x_recv, h_send, h_recv, r_send, r_recv,
 ):
@@ -293,11 +293,11 @@
     load_codes.wait()
 
     def product(m, carry):
-        at_row = pl.multiple_of(m * 256, 256)
-        keys[pl.ds(at_row, 256), :] = dot(codes[pl.ds(at_row, 256), :], signs[...])
+        at_row = pl.multiple_of(m * 512, 512)
+        keys[pl.ds(at_row, 512), :] = dot(codes[pl.ds(at_row, 512), :], signs[...])
         return carry
 
-    lax.fori_loop(0, 8, product, 0)
+    lax.fori_loop(0, 4, product, 0)
     sub = iota((8, 128), 0)
 
     def select(t):
@@ -341,13 +341,17 @@
     own_pos = jnp.where(iota((16, 16), 0) == iota((16, 16), 1), 1.0, 0.0)
     q_unit, q_hi, q_lo = unit[0:16], u_hi[0:16], u_lo[0:16]
 
+    u_qq[0:16], u_qq[16:32] = q_hi, q_lo
+    u_qqq[0:16], u_qqq[16:32], u_qqq[32:48] = q_hi, q_hi, q_lo
+
     def column(row):
         return jnp.sum(own_pos * jnp.broadcast_to(row, (16, 16)), axis=1, keepdims=True)
 
     def scores(start, count, mask):
         rows = slice(start, start + count)
         high, low = u_hi[rows], u_lo[rows]
-        logits = 50.0 * (dot(high, q_hi, LAST) + (dot(low, q_hi, LAST) + dot(high, q_lo, LAST)))
+        twice = dot(high, u_qq[...], LAST)
+        logits = 50.0 * (twice[:, 0:16] + (dot(low, q_hi, LAST) + twice[:, 16:32]))
         logits = jnp.where(mask > 0.5, logits, 0.0)
         return logits, jnp.where(mask > 0.5, jnp.exp(logits), 0.0)
 
@@ -359,20 +363,24 @@
         along = dot(w_hi, high, firsts) + (dot(w_lo, high, firsts) + dot(w_hi, low, firsts))
         scale = inv[rows, 0:1]
         k_hi, k_lo = split(w * (50.0 * scale))
-        pull = dot(k_hi, q_hi) + (dot(k_lo, q_hi) + dot(k_hi, q_lo))
+        pull = dot(jnp.concatenate([k_hi, k_lo, k_hi], axis=1), u_qqq[...])
         k2 = jnp.sum(w * logits, axis=1, keepdims=True) * scale
         raw[start - 32 : start - 32 + count] = pull - unit[rows] * k2
         return jnp.sum(w, axis=0, keepdims=True), along
 
+    select(0)
+    select(1)
     take(brecv.at[pl.ds(0, GROUP - 1)], b_sem.at[1])
     got = brecv[...].astype(F32)
     xs[32:288, 0:512] = got[:, 0:8].reshape(256, 512).astype(BF16)
     xs[32:288, 512:1024] = got[:, 8:16].reshape(256, 512).astype(BF16)
     project(32, 256)
     pass_on(2)
+    select(2)
     pos_logits, pos_w = scores(16, 16, own_pos)
     base_sum, base_along = negatives(32, 256)
     pass_on(1)
+    select(3)
     pass_on(3)
 
     take(r2a.at[0], x_recv.at[0, 0])
@@ -383,6 +391,9 @@
     xs[288:320, 0:512] = total(own_left, r3a).astype(BF16)
     take(r3b, x_recv.at[1, 4])
     xs[288:320, 512:1024] = total(own_right, r3b).astype(BF16)
+    for peer in others:
+        copy_to(shard_best.at[lax.div(peer, 8)], crecv.at[me], t_sem.at[0], t_sem.at[1], (z, peer)).start()
+    crecv[me] = shard_best[lax.div(me, 8)]
     project(288, 32)
     ext_sum, ext_along = negatives(288, 32)
 
@@ -453,14 +464,7 @@
     gather_core(1)
     grow(3)
     gather_core(2)
-    select(0)
     gather_core(3)
-    select(1)
-    select(2)
-    select(3)
-    for peer in others:
-        copy_to(shard_best.at[lax.div(peer, 8)], crecv.at[me], t_sem.at[0], t_sem.at[1], (z, peer)).start()
-    crecv[me] = shard_best[lax.div(me, 8)]
 
     out_v[8:40] = dot(dz[0:32], head[...], LAST)
 
@@ -600,6 +604,8 @@
             pltpu.VMEM((320, 128), F32),
             pltpu.VMEM((320, 1024), BF16),
             pltpu.VMEM((320, 1024), BF16),
+            pltpu.VMEM((32, 1024), BF16),
+            pltpu.VMEM((48, 1024), BF16),
             pltpu.VMEM((2, 4, 4, 4, 16, 512), BF16),
             pltpu.VMEM((4, 4, 4, 16, 512), BF16),
             pltpu.VMEM((4, 4, 4, 16, 512), BF16),

time: 53.7 us -> 54.1 us (level); the launches traced: 53.6 us -> 53.3 us
  no operation moved by 1% of the time
where the time goes in v6:
time: 54.1 us; the launch traced here: 53.3 us
  Pallas kernels  52.5 us (97%)
  between operations  0.8 us (1%)
    pallas_call x1, Pallas kernels, whole(): pl.pallas_call(whole_kernel, out_shape=jax.ShapeDtypeStruct((56, 1024), F...  50.9 us
    pallas_call x1, Pallas kernels, emit(): pl.pallas_call(emit_kernel, out_shape=tuple((jax.ShapeDtypeStruct(*o) for...  1.63 us

profile of v6, /device:TPU:1, one launch (start us, length us, event | category | flops | bytes accessed | tf_op | source)
XLA Modules:
  0.0 53.3 jit_solution(894235975934341420)
XLA Ops:
  0.6 50.9 %whole.1.packed_ref = f32[56,1024]{1,0:T(8,128)} custom-call(s32[16,64]{1,0:T(8,128)} %qcodes_hbm.1, s32[1,16]{1,0:T(1,128)} %bitcast.1, s32[16,16]{1,0:T(8,128)} %neg_hbm.1, bf16[2048,1024]{1,0:T(8,128)(2,1)} %codes_hbm.1, bf16[2048,1024]{1,0:T(8,128)(2,1)} %bank_hbm.1, bf16[16,1024]{1,0:T(8,128)(2,1)} %query_hbm.1, bf16[16,1024]{1,0:T(8,128)(2,1)} %positive_hbm.1, ...), custom_call_target="tpu_custom_call" | custom-call | tf_op jit(solution)/shard_map/whole/pallas_call | solution.py:564
  51.5 1.6 %emit.1 = (s32[16,16]{1,0:T(8,128)}, s32[16,16]{1,0:T(8,128)}, bf16[16,1024]{1,0:T(8,128)(2,1)}, bf16[16,1024]{1,0:T(8,128)(2,1)}, f32[8,1024]{1,0:T(8,128)}) custom-call(f32[56,1024]{1,0:T(8,128)} %whole.1.packed_ref), custom_call_target="tpu_custom_call" | custom-call | tf_op jit(solution)/shard_map/emit/pallas_call | solution.py:655

commit v7 on v6

--- a/solution.py
+++ b/solution.py
@@ -168,7 +168,7 @@
     qcodes_hbm, pos_hbm, neg_hbm, codes_hbm, bank_hbm, query_hbm, positive_hbm, head_hbm,
     out_hbm,
     qcodes, pos_in, neg_in, out_v,
-    bank, codes, head, pay, owned, out_buf, in_buf, bsend, brecv, esend, eown, ecore, s1, r2a, r2b, s2a, s2b, r3a, r3b,
+    bank, codes, head, pay, owned, out_buf, in_buf, bsend, brecv, esend, eown, ecore, s1, relay, both, r2a, r2b, s2a, s2b, r3a, r3b,
     signs, keys, pos, shard_best, crecv, packed, square, xs, dz, raw, unit, inv, u_hi, u_lo, u_qq, u_qqq,
     hs, core_in, parts, in1, mid, in2, tail, in3,
     load_sem, small_sem, p_sem, b_sem, t_sem, c_sem, x_send, x_recv, h_send, h_recv, r_send, r_recv,
@@ -267,17 +267,47 @@
     core_copy.wait_recv()
     s1[...] = (eown[...].astype(F32) + ecore[...].astype(F32)).astype(BF16).reshape(4, 4, 32, 1024)
 
-    left, right = pl.ds(0, 512), pl.ds(512, 512)
+    x1, x2, x3 = (lax.rem(x + k, SIDE) for k in (1, 2, 3))
+    y1, y2, y3 = (lax.rem(y + k, SIDE) for k in (1, 2, 3))
+    quarter = [pl.ds(256 * i, 256) for i in range(4)]
+    next_x, last_x = (z, at(x1, y, c)), (z, at(x3, y, c))
+    next_y, last_y = (z, at(x, y1, c)), (z, at(x, y3, c))
+    copy_to(s1.at[x2, :, :, quarter[0]], relay.at[0], x_send.at[0, 5], x_recv.at[0, 5], next_x).start()
+    copy_to(s1.at[:, y2, :, quarter[2]], relay.at[2], x_send.at[1, 5], x_recv.at[1, 5], next_y).start()
+    copy_to(s1.at[x2, :, :, quarter[1]], relay.at[1], x_send.at[0, 6], x_recv.at[0, 6], last_x).start()
+    copy_to(s1.at[:, y2, :, quarter[3]], relay.at[3], x_send.at[1, 6], x_recv.at[1, 6], last_y).start()
+
+    def send_two(j, sources):
+        for source, got, half, i, to in zip(
+            sources[0], (r2a.at[j, 0], r2a.at[j, 1], r2b.at[j, 0], r2b.at[j, 1]), sources[1], (0, 0, 1, 1),
+            (next_x, last_x, next_y, last_y),
+        ):
+            copy_to(source, got.at[:, quarter[half]], x_send.at[i, j], x_recv.at[i, j], to).start()
+
     for j in (2, 1, 3, 0):
         xj, yj = lax.rem(x + j, SIDE), lax.rem(y + j, SIDE)
-        for k in (2, 1, 3):
-            xk, yk = lax.rem(x + k, SIDE), lax.rem(y + k, SIDE)
-            copy_to(
-                s1.at[xk, yj, :, left], r2a.at[j, k - 1], x_send.at[0, j], x_recv.at[0, j], (z, at(xk, y, c))
-            ).start()
-            copy_to(
-                s1.at[xj, yk, :, right], r2b.at[j, k - 1], x_send.at[1, j], x_recv.at[1, j], (z, at(x, yk, c))
-            ).start()
+        plain = (
+            s1.at[x1, yj, :, quarter[1]],
+            s1.at[x3, yj, :, quarter[0]],
+            s1.at[xj, y1, :, quarter[3]],
+            s1.at[xj, y3, :, quarter[2]],
+        )
+        send_two(j, (plain, (1, 0, 1, 0)))
+
+    def relayed():
+        for i, own in enumerate(
+            (
+                lambda: s1[x1, :, :, 0:256],
+                lambda: s1[x3, :, :, 256:512],
+                lambda: s1[:, y1, :, 512:768],
+                lambda: s1[:, y3, :, 768:1024],
+            )
+        ):
+            take(relay.at[i], x_recv.at[i // 2, 5 + i % 2])
+            both[i] = (own().astype(F32) + relay[i].astype(F32)).astype(BF16)
+        for j in (2, 1, 3, 0):
+            xj, yj = lax.rem(x + j, SIDE), lax.rem(y + j, SIDE)
+            send_two(j, ((both.at[0, yj], both.at[1, yj], both.at[2, xj], both.at[3, xj]), (0, 1, 0, 1)))
 
     pairs = in_buf[:, 8:16, :]
     signs[...] = sign_rows(
@@ -298,6 +328,7 @@
         return carry
 
     lax.fori_loop(0, 4, product, 0)
+    relayed()
     sub = iota((8, 128), 0)
 
     def select(t):
@@ -322,19 +353,19 @@
         for i in range(16):
             shard_best[t, i : i + 1, :] = best[i][0:1, :]
 
-    def total(own, got):
+    def total(own, got, count=SIDE - 1):
         t = own.astype(F32)
-        for k in range(SIDE - 1):
+        for k in range(count):
             t = t + got[k].astype(F32)
         return t
 
     def pass_on(j):
         xj, yj = lax.rem(x + j, SIDE), lax.rem(y + j, SIDE)
         take(r2a.at[j], x_recv.at[0, j])
-        s2a[j] = total(s1[x, yj, :, 0:512], r2a.at[j]).astype(BF16)
+        s2a[j] = total(s1[x, yj, :, 0:512], r2a.at[j], 2).astype(BF16)
         copy_to(s2a.at[j], r3a.at[j - 1], x_send.at[0, 4], x_recv.at[0, 4], (z, at(x, yj, c))).start()
         take(r2b.at[j], x_recv.at[1, j])
-        s2b[j] = total(s1[xj, y, :, 512:1024], r2b.at[j]).astype(BF16)
+        s2b[j] = total(s1[xj, y, :, 512:1024], r2b.at[j], 2).astype(BF16)
         copy_to(s2b.at[j], r3b.at[j - 1], x_send.at[1, 4], x_recv.at[1, 4], (z, at(xj, y, c))).start()
 
     firsts = (((0,), (0,)), ((), ()))
@@ -384,9 +415,9 @@
     pass_on(3)
 
     take(r2a.at[0], x_recv.at[0, 0])
-    own_left = total(s1[x, y, :, 0:512], r2a.at[0])
+    own_left = total(s1[x, y, :, 0:512], r2a.at[0], 2)
     take(r2b.at[0], x_recv.at[1, 0])
-    own_right = total(s1[x, y, :, 512:1024], r2b.at[0])
+    own_right = total(s1[x, y, :, 512:1024], r2b.at[0], 2)
     take(r3a, x_recv.at[0, 4])
     xs[288:320, 0:512] = total(own_left, r3a).astype(BF16)
     take(r3b, x_recv.at[1, 4])
@@ -541,6 +572,8 @@
     for j in range(SIDE):
         take(r2a.at[j], x_send.at[0, j])
         take(r2b.at[j], x_send.at[1, j])
+    for i in range(4):
+        take(relay.at[i], x_send.at[i // 2, 5 + i % 2])
     take(r3a, x_send.at[0, 4])
     take(r3b, x_send.at[1, 4])
     take(core_in, h_send)
@@ -584,8 +617,10 @@
             pltpu.VMEM((16, 32, 1024), BF16),
             pltpu.VMEM((16, 32, 1024), BF16),
             pltpu.VMEM((4, 4, 32, 1024), BF16),
-            pltpu.VMEM((4, 3, 32, 512), BF16),
-            pltpu.VMEM((4, 3, 32, 512), BF16),
+            pltpu.VMEM((4, 4, 32, 256), BF16),
+            pltpu.VMEM((4, 4, 32, 256), BF16),
+            pltpu.VMEM((4, 2, 32, 512), BF16),
+            pltpu.VMEM((4, 2, 32, 512), BF16),
             pltpu.VMEM((4, 32, 512), BF16),
             pltpu.VMEM((4, 32, 512), BF16),
             pltpu.VMEM((3, 32, 512), BF16),
@@ -620,8 +655,8 @@
             dma((2,)),
             dma((2,)),
             dma((2,)),
-            dma((2, 5)),
-            dma((2, 5)),
+            dma((2, 7)),
+            dma((2, 7)),
             dma,
             dma((4,)),
             dma((3, 5)),

time: 54.1 us -> 55.5 us (1.026)
  Pallas kernels: 52.5 us -> 54 us
    pallas_call x1, Pallas kernels: 50.9 us -> 52.4 us  [whole(): pl.pallas_call(whole_kernel, out_shape=jax.ShapeDtypeStruct((56, 1024), F...]
where the time goes in v7:
time: 55.5 us; the launch traced here: 54.8 us
  Pallas kernels  54 us (97%)
  between operations  0.8 us (1%)
    pallas_call x1, Pallas kernels, whole(): pl.pallas_call(whole_kernel, out_shape=jax.ShapeDtypeStruct((56, 1024), F...  52.4 us
    pallas_call x1, Pallas kernels, emit(): pl.pallas_call(emit_kernel, out_shape=tuple((jax.ShapeDtypeStruct(*o) for...  1.63 us

profile of v7, /device:TPU:1, one launch (start us, length us, event | category | flops | bytes accessed | tf_op | source)
XLA Modules:
  0.0 54.8 jit_solution(17060389934189494170)
XLA Ops:
  0.6 52.4 %whole.1.packed_ref = f32[56,1024]{1,0:T(8,128)} custom-call(s32[16,64]{1,0:T(8,128)} %qcodes_hbm.1, s32[1,16]{1,0:T(1,128)} %bitcast.1, s32[16,16]{1,0:T(8,128)} %neg_hbm.1, bf16[2048,1024]{1,0:T(8,128)(2,1)} %codes_hbm.1, bf16[2048,1024]{1,0:T(8,128)(2,1)} %bank_hbm.1, bf16[16,1024]{1,0:T(8,128)(2,1)} %query_hbm.1, bf16[16,1024]{1,0:T(8,128)(2,1)} %positive_hbm.1, ...), custom_call_target="tpu_custom_call" | custom-call | tf_op jit(solution)/shard_map/whole/pallas_call | solution.py:597
  53.1 1.6 %emit.1 = (s32[16,16]{1,0:T(8,128)}, s32[16,16]{1,0:T(8,128)}, bf16[16,1024]{1,0:T(8,128)(2,1)}, bf16[16,1024]{1,0:T(8,128)(2,1)}, f32[8,1024]{1,0:T(8,128)}) custom-call(f32[56,1024]{1,0:T(8,128)} %whole.1.packed_ref), custom_call_target="tpu_custom_call" | custom-call | tf_op jit(solution)/shard_map/emit/pallas_call | solution.py:690

commit v8 on v6

--- a/solution.py
+++ b/solution.py
@@ -319,8 +319,14 @@
         best = lax.fori_loop(1, 16, step, tuple(sort16(load16(0))))
         for d in (4, 2, 1):
             best = merge16(best, [pltpu.roll(b, d, 0) for b in best])
-        for i in range(16):
-            shard_best[t, i : i + 1, :] = best[i][0:1, :]
+        low, high = best[0], best[8]
+        for i in range(1, 8):
+            low = jnp.where(sub == i, best[i], low)
+            high = jnp.where(sub == i, best[8 + i], high)
+        high = pltpu.roll(high, 64, 1)
+        left_half = iota((8, 128), 1) < 64
+        shard_best[t, 0] = jnp.where(left_half, low, high)
+        shard_best[t, 1] = jnp.where(left_half, high, low)
 
     def total(own, got):
         t = own.astype(F32)
@@ -368,19 +374,15 @@
         raw[start - 32 : start - 32 + count] = pull - unit[rows] * k2
         return jnp.sum(w, axis=0, keepdims=True), along
 
-    select(0)
-    select(1)
     take(brecv.at[pl.ds(0, GROUP - 1)], b_sem.at[1])
     got = brecv[...].astype(F32)
     xs[32:288, 0:512] = got[:, 0:8].reshape(256, 512).astype(BF16)
     xs[32:288, 512:1024] = got[:, 8:16].reshape(256, 512).astype(BF16)
     project(32, 256)
     pass_on(2)
-    select(2)
     pos_logits, pos_w = scores(16, 16, own_pos)
     base_sum, base_along = negatives(32, 256)
     pass_on(1)
-    select(3)
     pass_on(3)
 
     take(r2a.at[0], x_recv.at[0, 0])
@@ -391,9 +393,6 @@
     xs[288:320, 0:512] = total(own_left, r3a).astype(BF16)
     take(r3b, x_recv.at[1, 4])
     xs[288:320, 512:1024] = total(own_right, r3b).astype(BF16)
-    for peer in others:
-        copy_to(shard_best.at[lax.div(peer, 8)], crecv.at[me], t_sem.at[0], t_sem.at[1], (z, peer)).start()
-    crecv[me] = shard_best[lax.div(me, 8)]
     project(288, 32)
     ext_sum, ext_along = negatives(288, 32)
 
@@ -464,7 +463,11 @@
     gather_core(1)
     grow(3)
     gather_core(2)
+    select(0)
     gather_core(3)
+    select(1)
+    select(2)
+    select(3)
 
     out_v[8:40] = dot(dz[0:32], head[...], LAST)
 
@@ -482,6 +485,13 @@
             copy_to(
                 mid[p].at[pick(p, 1, to)], in2[p].at[k - 1], r_send.at[1, p], r_recv.at[1, p], device(axis, to)
             ).start()
+    def half_of(device):
+        return lax.div(device, 8), lax.div(lax.rem(device, 8), 4)
+
+    for peer in others:
+        copy_to(shard_best.at[half_of(peer)], crecv.at[me], t_sem.at[0], t_sem.at[1], (z, peer)).start()
+    crecv[me] = shard_best[half_of(me)]
+
     for p in (1, 2, 4, 0, 3):
         axis = PORTIONS[p][3][1]
         take(in2[p], r_recv.at[1, p])
@@ -507,7 +517,8 @@
     for g in range(4):
         merged = jnp.zeros((16, 128), jnp.int32)
         for s in range(8):
-            key = crecv[g * 8 + s].astype(jnp.int32)
+            got = crecv[g * 8 + s]
+            key = jnp.concatenate([got, pltpu.roll(got, 64, 1)], axis=0).astype(jnp.int32)
             key = ((key >> 11) << 16) + (key & 2047) + (g * 8 + s) * 2048
             key = pltpu.roll(key, lax.rem((s - mine + 8) * 16, 128), 1)
             merged = jnp.where((lane >> 4) == s, key, merged)
@@ -593,8 +604,8 @@
             pltpu.VMEM((1024, 512), BF16),
             pltpu.VMEM((2048, 512), F32),
             pltpu.VMEM((8, 512), F32),
-            pltpu.VMEM((4, 16, 128), F32),
-            pltpu.VMEM((32, 16, 128), F32),
+            pltpu.VMEM((4, 2, 8, 128), F32),
+            pltpu.VMEM((32, 8, 128), F32),
             pltpu.VMEM((8, 16, 128), jnp.int32),
             pltpu.VMEM((128, 128), jnp.int32),
             pltpu.VMEM((320, 1024), BF16),

time: 54.1 us -> 52.5 us (0.970); the launches traced: 53.3 us -> 52.3 us
  Pallas kernels: 52.5 us -> 51.5 us
    pallas_call x1, Pallas kernels: 50.9 us -> 49.9 us  [whole(): pl.pallas_call(whole_kernel, out_shape=jax.ShapeDtypeStruct((56, 1024), F...]
where the time goes in v8:
time: 52.5 us; the launch traced here: 52.3 us
  Pallas kernels  51.5 us (98%)
  between operations  0.8 us (2%)
    pallas_call x1, Pallas kernels, whole(): pl.pallas_call(whole_kernel, out_shape=jax.ShapeDtypeStruct((56, 1024), F...  49.9 us
    pallas_call x1, Pallas kernels, emit(): pl.pallas_call(emit_kernel, out_shape=tuple((jax.ShapeDtypeStruct(*o) for...  1.63 us

profile of v8, /device:TPU:1, one launch (start us, length us, event | category | flops | bytes accessed | tf_op | source)
XLA Modules:
  0.0 52.3 jit_solution(8601382804073968859)
XLA Ops:
  0.6 49.9 %whole.1.packed_ref = f32[56,1024]{1,0:T(8,128)} custom-call(s32[16,64]{1,0:T(8,128)} %qcodes_hbm.1, s32[1,16]{1,0:T(1,128)} %bitcast.1, s32[16,16]{1,0:T(8,128)} %neg_hbm.1, bf16[2048,1024]{1,0:T(8,128)(2,1)} %codes_hbm.1, bf16[2048,1024]{1,0:T(8,128)(2,1)} %bank_hbm.1, bf16[16,1024]{1,0:T(8,128)(2,1)} %query_hbm.1, bf16[16,1024]{1,0:T(8,128)(2,1)} %positive_hbm.1, ...), custom_call_target="tpu_custom_call" | custom-call | tf_op jit(solution)/shard_map/whole/pallas_call | solution.py:575
  50.5 1.6 %emit.1 = (s32[16,16]{1,0:T(8,128)}, s32[16,16]{1,0:T(8,128)}, bf16[16,1024]{1,0:T(8,128)(2,1)}, bf16[16,1024]{1,0:T(8,128)(2,1)}, f32[8,1024]{1,0:T(8,128)}) custom-call(f32[56,1024]{1,0:T(8,128)} %whole.1.packed_ref), custom_call_target="tpu_custom_call" | custom-call | tf_op jit(solution)/shard_map/emit/pallas_call | solution.py:666

commit v9 on v6

--- a/solution.py
+++ b/solution.py
@@ -319,8 +319,14 @@
         best = lax.fori_loop(1, 16, step, tuple(sort16(load16(0))))
         for d in (4, 2, 1):
             best = merge16(best, [pltpu.roll(b, d, 0) for b in best])
-        for i in range(16):
-            shard_best[t, i : i + 1, :] = best[i][0:1, :]
+        low, high = best[0], best[8]
+        for i in range(1, 8):
+            low = jnp.where(sub == i, best[i], low)
+            high = jnp.where(sub == i, best[8 + i], high)
+        high = pltpu.roll(high, 64, 1)
+        left_half = iota((8, 128), 1) < 64
+        shard_best[t, 0] = jnp.where(left_half, low, high)
+        shard_best[t, 1] = jnp.where(left_half, high, low)
 
     def total(own, got):
         t = own.astype(F32)
@@ -391,9 +397,12 @@
     xs[288:320, 0:512] = total(own_left, r3a).astype(BF16)
     take(r3b, x_recv.at[1, 4])
     xs[288:320, 512:1024] = total(own_right, r3b).astype(BF16)
+    def half_of(device):
+        return lax.div(device, 8), lax.div(lax.rem(device, 8), 4)
+
     for peer in others:
-        copy_to(shard_best.at[lax.div(peer, 8)], crecv.at[me], t_sem.at[0], t_sem.at[1], (z, peer)).start()
-    crecv[me] = shard_best[lax.div(me, 8)]
+        copy_to(shard_best.at[half_of(peer)], crecv.at[me], t_sem.at[0], t_sem.at[1], (z, peer)).start()
+    crecv[me] = shard_best[half_of(me)]
     project(288, 32)
     ext_sum, ext_along = negatives(288, 32)
 
@@ -467,6 +476,33 @@
     gather_core(3)
 
     out_v[8:40] = dot(dz[0:32], head[...], LAST)
+
+    take(crecv.at[pl.ds(0, GROUP - 1)], t_sem.at[1])
+    lane = iota((16, 128), 1)
+    packed[...] = jnp.full((8, 16, 128), 2147483647, jnp.int32)
+    mine = lax.rem(me, 8)
+    for g in range(4):
+        merged = jnp.zeros((16, 128), jnp.int32)
+        for s in range(8):
+            got = crecv[g * 8 + s]
+            key = jnp.concatenate([got, pltpu.roll(got, 64, 1)], axis=0).astype(jnp.int32)
+            key = ((key >> 11) << 16) + (key & 2047) + (g * 8 + s) * 2048
+            key = pltpu.roll(key, lax.rem((s - mine + 8) * 16, 128), 1)
+            merged = jnp.where((lane >> 4) == s, key, merged)
+        packed[g] = merged
+    best = [packed[:, i, :] for i in range(16)]
+    for d in (64, 32, 16):
+        best = merge16(best, [pltpu.roll(b, d, 1) for b in best])
+    for d in (6, 7):
+        best = merge16(best, [pltpu.roll(b, d, 0) for b in best])
+    square[...] = jnp.zeros((128, 128), jnp.int32)
+    for i in range(16):
+        square[i : i + 1, :] = best[i][0:1, :]
+    flat = square[...]
+    out_v[40:56, 0:128] = jnp.transpose((flat & 65535).astype(F32))[0:16]
+    out_v[40:56, 128:256] = jnp.transpose((flat >> 16).astype(F32))[0:16]
+    early = pltpu.make_async_copy(out_v.at[pl.ds(8, 48)], out_hbm.at[pl.ds(8, 48)], small_sem.at[0])
+    early.start()
 
     def pick(p, stage, to):
         axis = PORTIONS[p][3][stage]
@@ -500,32 +536,6 @@
             copy_to(
                 tail.at[q, to], in3.at[q, k - 1], r_send.at[2, q], r_recv.at[2, q], device(axis, to)
             ).start()
-    take(crecv.at[pl.ds(0, GROUP - 1)], t_sem.at[1])
-    lane = iota((16, 128), 1)
-    packed[...] = jnp.full((8, 16, 128), 2147483647, jnp.int32)
-    mine = lax.rem(me, 8)
-    for g in range(4):
-        merged = jnp.zeros((16, 128), jnp.int32)
-        for s in range(8):
-            key = crecv[g * 8 + s].astype(jnp.int32)
-            key = ((key >> 11) << 16) + (key & 2047) + (g * 8 + s) * 2048
-            key = pltpu.roll(key, lax.rem((s - mine + 8) * 16, 128), 1)
-            merged = jnp.where((lane >> 4) == s, key, merged)
-        packed[g] = merged
-    best = [packed[:, i, :] for i in range(16)]
-    for d in (64, 32, 16):
-        best = merge16(best, [pltpu.roll(b, d, 1) for b in best])
-    for d in (6, 7):
-        best = merge16(best, [pltpu.roll(b, d, 0) for b in best])
-    square[...] = jnp.zeros((128, 128), jnp.int32)
-    for i in range(16):
-        square[i : i + 1, :] = best[i][0:1, :]
-    flat = square[...]
-    out_v[40:56, 0:128] = jnp.transpose((flat & 65535).astype(F32))[0:16]
-    out_v[40:56, 128:256] = jnp.transpose((flat >> 16).astype(F32))[0:16]
-    early = pltpu.make_async_copy(out_v.at[pl.ds(8, 48)], out_hbm.at[pl.ds(8, 48)], small_sem.at[0])
-    early.start()
-
     for q in range(4):
         take(in3.at[q], r_recv.at[2, q])
         out = total(tail[q, place[PORTIONS[q][3][2]]], in3.at[q])
@@ -593,8 +603,8 @@
             pltpu.VMEM((1024, 512), BF16),
             pltpu.VMEM((2048, 512), F32),
             pltpu.VMEM((8, 512), F32),
-            pltpu.VMEM((4, 16, 128), F32),
-            pltpu.VMEM((32, 16, 128), F32),
+            pltpu.VMEM((4, 2, 8, 128), F32),
+            pltpu.VMEM((32, 8, 128), F32),
             pltpu.VMEM((8, 16, 128), jnp.int32),
             pltpu.VMEM((128, 128), jnp.int32),
             pltpu.VMEM((320, 1024), BF16),

time: 54.1 us -> 54.4 us (level)
  no operation moved by 1% of the time
where the time goes in v9:
time: 54.4 us; the launch traced here: 53.5 us
  Pallas kernels  52.7 us (97%)
  between operations  0.8 us (1%)
    pallas_call x1, Pallas kernels, whole(): pl.pallas_call(whole_kernel, out_shape=jax.ShapeDtypeStruct((56, 1024), F...  51.1 us
    pallas_call x1, Pallas kernels, emit(): pl.pallas_call(emit_kernel, out_shape=tuple((jax.ShapeDtypeStruct(*o) for...  1.63 us

profile of v9, /device:TPU:1, one launch (start us, length us, event | category | flops | bytes accessed | tf_op | source)
XLA Modules:
  0.0 53.5 jit_solution(16054210045276974541)
XLA Ops:
  0.6 51.1 %whole.1.packed_ref = f32[56,1024]{1,0:T(8,128)} custom-call(s32[16,64]{1,0:T(8,128)} %qcodes_hbm.1, s32[1,16]{1,0:T(1,128)} %bitcast.1, s32[16,16]{1,0:T(8,128)} %neg_hbm.1, bf16[2048,1024]{1,0:T(8,128)(2,1)} %codes_hbm.1, bf16[2048,1024]{1,0:T(8,128)(2,1)} %bank_hbm.1, bf16[16,1024]{1,0:T(8,128)(2,1)} %query_hbm.1, bf16[16,1024]{1,0:T(8,128)(2,1)} %positive_hbm.1, ...), custom_call_target="tpu_custom_call" | custom-call | tf_op jit(solution)/shard_map/whole/pallas_call | solution.py:574
  51.8 1.6 %emit.1 = (s32[16,16]{1,0:T(8,128)}, s32[16,16]{1,0:T(8,128)}, bf16[16,1024]{1,0:T(8,128)(2,1)}, bf16[16,1024]{1,0:T(8,128)(2,1)}, f32[8,1024]{1,0:T(8,128)}) custom-call(f32[56,1024]{1,0:T(8,128)} %whole.1.packed_ref), custom_call_target="tpu_custom_call" | custom-call | tf_op jit(solution)/shard_map/emit/pallas_call | solution.py:665
